TPU v7x, 128 devices: a whole 4x4x4 slice. The times are simulated.
128 devices in a mesh: row: 16 (over x_hi, y, core), col: 8 (over z, x_lo).
Axes of the slice: x: 4 (x_hi: 2, x_lo: 2; x = x_hi * 2 + x_lo), y: 4, z: 4, core: 2. Of those that a mesh axis runs over, the one named last changes fastest.
Arguments:
- children: bfloat16 [8, 16, 256, 8, 8, 256], P(None, 'row', None, None, 'col'), may hold values from -1 to 8193
- child_maps: int32 [2, 64], replicated, may hold values from 0 to 102, as said below
- coupling: bfloat16 [7, 16, 256, 1024], P(None, 'row'), may hold values from -48 to 48
- pivot_shift: float32 [1024], replicated, may hold values from 1280 to 2304
Outputs:
- factored_front: bfloat16 [7, 16, 256, 14, 8, 256], P(None, 'row', None, None, 'col')
Inputs may be any that keep to these rules, and one draw needn't show every extreme that they name: Each child_maps[h] is strictly increasing. child_maps[0, t] = t for t < 4, and every other entry is 4 or more. For every h and every q < 8, at most 1 of the tiles child_maps[h, a * 8 + q] (a < 8) share a remainder modulo 2 * 8; for every c < 8, at most 1 of the tiles child_maps[h, b * 8 + c] (b < 8) share a remainder modulo 8. Both bounds are reached.
All inputs are finite; a program needn't handle non-finite values.
Results may differ from a plain program's by a relative error of at most 0.0048.
The roundings to bfloat16 on the way count: a program that leaves them out, or rounds other values in their place, can miss the bound.
Values may be sent and summed in bfloat16 or wider, within the bound.
No kernel may reach another device: no remote copies, remote signals or barrier semaphores. Data moves between devices by JAX's collectives and lax.ppermute only.
A program may use at most 192 MiB of HBM per device.

v0:
```python
import jax
import jax.numpy as jnp
from jax import lax
from jax.sharding import PartitionSpec as P

NT = 112


def from_root(shard, axis, root):
    mine = lax.axis_index(axis) == root
    return lax.psum(jnp.where(mine, shard, jnp.zeros_like(shard)), axis)


def earlier_same(dest_ids):
    positions = jnp.arange(dest_ids.shape[0])
    same_dest = dest_ids[:, None] == dest_ids[None, :]
    before = positions[:, None] > positions[None, :]
    return jnp.sum(jnp.where(same_dest & before, 1, 0), axis=1).astype(jnp.int32)


def pick_slots(dest_ids, rank_ids, group_count, slot_count):
    matched = (dest_ids[None, None, :] == jnp.arange(group_count)[:, None, None]) & (
        rank_ids[None, None, :] == jnp.arange(slot_count)[None, :, None]
    )
    item_ids = jnp.arange(dest_ids.shape[0])
    chosen = jnp.sum(jnp.where(matched, item_ids[None, None, :], 0), axis=2)
    present = jnp.any(matched, axis=2)
    return (chosen, present)


def landing(
    child_maps,
    rows_grid,
    cols_grid,
    my_row,
    my_col,
    row_tiles,
    col_tiles,
    cap_rows,
    cap_cols,
    local_cols,
):
    half_rows = rows_grid // 2
    sources = jnp.arange(rows_grid)
    source_side = sources // half_rows
    source_within = sources % half_rows
    row_ids = jnp.arange(row_tiles)[None, :] * half_rows + source_within[:, None]
    row_target = jnp.take_along_axis(child_maps[source_side], row_ids, axis=1)
    row_hit = row_target % rows_grid == my_row
    row_rank = jnp.cumsum(row_hit.astype(jnp.int32), axis=1) - 1
    row_sel = row_hit[:, :, None] & (row_rank[:, :, None] == jnp.arange(cap_rows)[None, None, :])
    parent_row = jnp.sum(jnp.where(row_sel, (row_target // rows_grid)[:, :, None], 0), axis=1)
    row_valid = jnp.any(row_sel, axis=1)
    col_ids = jnp.arange(col_tiles)[None, :] * cols_grid + jnp.arange(cols_grid)[:, None]
    col_target = child_maps[:, col_ids]
    col_hit = col_target % cols_grid == my_col
    col_rank = jnp.cumsum(col_hit.astype(jnp.int32), axis=2) - 1
    col_sel = col_hit[..., None] & (col_rank[..., None] == jnp.arange(cap_cols))
    parent_col = jnp.sum(jnp.where(col_sel, (col_target // cols_grid)[..., None], 0), axis=2)[
        source_side
    ]
    col_valid = jnp.any(col_sel, axis=2)[source_side]
    target = parent_row[:, None, :, None] * local_cols + parent_col[:, :, None, :]
    valid = row_valid[:, None, :, None] & col_valid[:, :, None, :]
    return (target, valid)


def per_device(children, child_maps, coupling, pivot_shift):
    rows_grid = lax.axis_size("row")
    cols_grid = lax.axis_size("col")
    half_rows = rows_grid // 2
    my_row = lax.axis_index("row")
    my_col = lax.axis_index("col")
    row_tiles = children.shape[0]
    tile_size = children.shape[2]
    col_tiles = children.shape[3]
    local_rows = coupling.shape[0]
    width = coupling.shape[3]
    panels = width // tile_size
    local_cols = NT // cols_grid
    local_count = local_rows * local_cols
    cap_rows = (row_tiles + rows_grid - 1) // rows_grid
    cap_cols = (col_tiles + cols_grid - 1) // cols_grid
    own_map = child_maps[my_row // half_rows]
    send_rows = own_map[jnp.arange(row_tiles) * half_rows + my_row % half_rows]
    send_cols = own_map[jnp.arange(col_tiles) * cols_grid + my_col]
    row_dest = send_rows % rows_grid
    col_dest = send_cols % cols_grid
    pick_rows, have_rows = pick_slots(row_dest, earlier_same(row_dest), rows_grid, cap_rows)
    pick_cols, have_cols = pick_slots(col_dest, earlier_same(col_dest), cols_grid, cap_cols)
    target, valid = landing(
        child_maps,
        rows_grid,
        cols_grid,
        my_row,
        my_col,
        row_tiles,
        col_tiles,
        cap_rows,
        cap_cols,
        local_cols,
    )
    tile_block = children.reshape(row_tiles, tile_size, col_tiles, tile_size)
    slot_of = jnp.arange(local_count)
    chosen = tile_block[pick_rows[:, None, :, None], :, pick_cols[None, :, None, :], :]
    keep = have_rows[:, None, :, None] & have_cols[None, :, None, :]
    chosen = jnp.where(keep[..., None, None], chosen, jnp.zeros((), children.dtype))
    outgoing = chosen.reshape(rows_grid * cols_grid, cap_rows, cap_cols, tile_size, tile_size)
    incoming = lax.all_to_all(outgoing, ("row", "col"), split_axis=0, concat_axis=0, tiled=True)
    onehot = (target.reshape(-1)[None, :] == slot_of[:, None]) & valid.reshape(-1)[None, :]
    assembled = jnp.dot(
        onehot.astype(jnp.bfloat16),
        incoming.reshape(-1, tile_size * tile_size),
        preferred_element_type=jnp.float32,
    )
    front = jnp.transpose(
        assembled.reshape(local_rows, local_cols, tile_size, tile_size), (0, 2, 1, 3)
    ).reshape(local_rows * tile_size, local_cols * tile_size)
    row_tile_of = jnp.repeat(jnp.arange(local_rows) * rows_grid + my_row, tile_size)
    col_tile_of = jnp.repeat(jnp.arange(local_cols) * cols_grid + my_col, tile_size)
    pivot_index = jnp.minimum(my_col, panels - 1)
    strip_rows = coupling.reshape(local_rows * tile_size, width)
    added_cols = lax.dynamic_slice_in_dim(strip_rows, pivot_index * tile_size, tile_size, 1).astype(
        jnp.float32
    )
    added_cols = jnp.where((row_tile_of[:, None] >= panels) & (my_col < panels), added_cols, 0.0)
    front = front.at[:, 0:tile_size].add(added_cols)
    shift_part = lax.dynamic_slice_in_dim(pivot_shift, pivot_index * tile_size, tile_size, 0)
    on_diagonal = (my_row == my_col) & (my_col < panels)
    front = front.at[0:tile_size, 0:tile_size].add(
        jnp.where(on_diagonal, jnp.diag(shift_part), 0.0)
    )
    for panel_step in range(panels):
        pivot_tile = from_root(front[0:tile_size, 0:tile_size], "row", panel_step)
        symmetric = jnp.tril(pivot_tile) + jnp.transpose(jnp.tril(pivot_tile, -1))
        factor = jnp.linalg.cholesky(symmetric)
        column = front[:, 0:tile_size]
        solved = jnp.transpose(
            jax.scipy.linalg.solve_triangular(factor, jnp.transpose(column), lower=True)
        )
        panel_cols = jnp.where(row_tile_of[:, None] > panel_step, solved, 0.0)
        top_rows = jnp.where(my_row == panel_step, factor, panel_cols[0:tile_size])
        panel_cols = panel_cols.at[0:tile_size].set(top_rows)
        panel_low = from_root(panel_cols.astype(jnp.bfloat16), "col", panel_step)
        pieces = []
        for owner_step in range(rows_grid // cols_grid):
            received = from_root(panel_low, "row", my_col + owner_step * cols_grid)
            pieces.append(received.reshape(local_rows, tile_size, tile_size))
        across = jnp.stack(pieces, axis=1).reshape(local_cols * tile_size, tile_size)
        update = jnp.einsum("ik,jk->ij", panel_low, across, preferred_element_type=jnp.float32)
        trailing = (row_tile_of[:, None] > panel_step) & (col_tile_of[None, :] > panel_step)
        front = jnp.where(trailing, front - update, front)
        front = front.at[:, 0:tile_size].set(
            jnp.where(my_col == panel_step, panel_low.astype(jnp.float32), front[:, 0:tile_size])
        )
    upper_part = (row_tile_of[:, None] < panels) & (col_tile_of[None, :] >= panels)
    result = jnp.where(upper_part, 0.0, front).astype(jnp.bfloat16)
    return result.reshape(local_rows, 1, tile_size, local_cols, 1, tile_size)


def solution(mesh):
    in_specs = (P(None, "row", None, None, "col", None), P(), P(None, "row", None, None), P())
    out_specs = P(None, "row", None, None, "col", None)
    return jax.shard_map(
        per_device, mesh=mesh, in_specs=in_specs, out_specs=out_specs, check_vma=False
    )
```

profile of v0, /device:TPU:8, one launch (start us, length us, event | category | flops | bytes accessed | tf_op | source)
XLA Modules:
  0.0 2228.6 jit_solution(2411516478983601571)
XLA Ops:
  63.1 224.0 %all-to-all-done = bf16[128,1,1,256,256]{4,3,2,1,0:T(8,128)(2,1)} async-done(((bf16[128,1,1,256,256]{4,3,2,1,0:T(8,128)(2,1)}), bf16[128,1,1,256,256]{4,3,2,1,0:T(8,128)(2,1)}, u32[]{:S(2)}, u32[]{:S(2)}) %all-to-all-start) | async-done | bytes 16777248 | tf_op jit(solution)/shard_map/all_to_all | solution.py:109
  287.1 23.8 %copy.103 = bf16[128,1,1,256,256]{0,4,3,2,1:T(8,128)(2,1)} copy(bf16[128,1,1,256,256]{4,3,2,1,0:T(8,128)(2,1)} %all-to-all-done) | data formatting | bytes 33554432 | tf_op jit(solution)/shard_map/all_to_all | solution.py:109
  310.9 16.2 fusion
  327.1 24.5 %copy.159 = f32[224,8,14,256]{3,1,2,0:T(8,128)} copy(f32[224,8,14,256]{3,2,1,0:T(8,128)} %bitcast.256) | data formatting | bytes 51380224
  358.2 129.9 %all-reduce.18.cloned.1.call-done = f32[256,256]{1,0:T(8,128)} async-done(((f32[256,256]{1,0:T(8,128)}), f32[256,256]{1,0:T(8,128)}) %all-reduce.18.cloned.1.call-update) | async-done | bytes 262160 | tf_op jit(solution)/shard_map/psum | solution.py:11
  531.6 19.7 custom-call.22
  559.0 85.3 %all-reduce.20.cloned.1.call-done = bf16[1792,256]{1,0:T(8,128)(2,1)} async-done(((bf16[1792,256]{1,0:T(8,128)(2,1)}), bf16[1792,256]{1,0:T(8,128)(2,1)}) %all-reduce.20.cloned.1.call-update) | async-done | bytes 917520 | tf_op jit(solution)/shard_map/psum | solution.py:11
  647.0 137.3 %all-reduce.40.cloned.1.call-done = (bf16[7,1,256,256]{3,2,1,0:T(8,128)(2,1)}, bf16[7,1,256,256]{3,2,1,0:T(8,128)(2,1)}) async-done(((bf16[7,1,256,256]{3,2,1,0:T(8,128)(2,1)}, bf16[7,1,256,256]{3,2,1,0:T(8,128)(2,1)}), (bf16[7,1,256,256]{3,2,1,0:T(8,128)(2,1)}, bf16[7,1,256,256]{3,2,1,0:T(8,128)(2,1)})) %all-reduce.40.cloned.1.call-update) | async-done | bytes 1835024 | tf_op jit(solution)/shard_map/psum | solution.py:11
  786.1 16.2 subtract_select_fusion.3
  807.1 138.6 %all-reduce.22.cloned.1.call-done = f32[256,256]{1,0:T(8,128)} async-done(((f32[256,256]{1,0:T(8,128)}), f32[256,256]{1,0:T(8,128)}) %all-reduce.22.cloned.1.call-update) | async-done | bytes 262160 | tf_op jit(solution)/shard_map/psum | solution.py:11
  988.6 19.7 custom-call.24
  1016.0 85.3 %all-reduce.24.cloned.1.call-done = bf16[1792,256]{1,0:T(8,128)(2,1)} async-done(((bf16[1792,256]{1,0:T(8,128)(2,1)}), bf16[1792,256]{1,0:T(8,128)(2,1)}) %all-reduce.24.cloned.1.call-update) | async-done | bytes 917520 | tf_op jit(solution)/shard_map/psum | solution.py:11
  1104.0 137.3 %all-reduce.38.cloned.1.call-done = (bf16[7,1,256,256]{3,2,1,0:T(8,128)(2,1)}, bf16[7,1,256,256]{3,2,1,0:T(8,128)(2,1)}) async-done(((bf16[7,1,256,256]{3,2,1,0:T(8,128)(2,1)}, bf16[7,1,256,256]{3,2,1,0:T(8,128)(2,1)}), (bf16[7,1,256,256]{3,2,1,0:T(8,128)(2,1)}, bf16[7,1,256,256]{3,2,1,0:T(8,128)(2,1)})) %all-reduce.38.cloned.1.call-update) | async-done | bytes 1835024 | tf_op jit(solution)/shard_map/psum | solution.py:11
  1243.0 16.2 subtract_select_fusion.2
  1264.2 138.3 %all-reduce.26.cloned.1.call-done = f32[256,256]{1,0:T(8,128)} async-done(((f32[256,256]{1,0:T(8,128)}), f32[256,256]{1,0:T(8,128)}) %all-reduce.26.cloned.1.call-update) | async-done | bytes 262160 | tf_op jit(solution)/shard_map/psum | solution.py:11
  1445.2 19.7 custom-call.26
  1472.6 85.3 %all-reduce.28.cloned.1.call-done = bf16[1792,256]{1,0:T(8,128)(2,1)} async-done(((bf16[1792,256]{1,0:T(8,128)(2,1)}), bf16[1792,256]{1,0:T(8,128)(2,1)}) %all-reduce.28.cloned.1.call-update) | async-done | bytes 917520 | tf_op jit(solution)/shard_map/psum | solution.py:11
  1560.7 137.3 %all-reduce.36.cloned.1.call-done = (bf16[7,1,256,256]{3,2,1,0:T(8,128)(2,1)}, bf16[7,1,256,256]{3,2,1,0:T(8,128)(2,1)}) async-done(((bf16[7,1,256,256]{3,2,1,0:T(8,128)(2,1)}, bf16[7,1,256,256]{3,2,1,0:T(8,128)(2,1)}), (bf16[7,1,256,256]{3,2,1,0:T(8,128)(2,1)}, bf16[7,1,256,256]{3,2,1,0:T(8,128)(2,1)})) %all-reduce.36.cloned.1.call-update) | async-done | bytes 1835024 | tf_op jit(solution)/shard_map/psum | solution.py:11
  1699.7 16.2 subtract_select_fusion.1
  1720.9 138.3 %all-reduce.30.cloned.1.call-done = f32[256,256]{1,0:T(8,128)} async-done(((f32[256,256]{1,0:T(8,128)}), f32[256,256]{1,0:T(8,128)}) %all-reduce.30.cloned.1.call-update) | async-done | bytes 262160 | tf_op jit(solution)/shard_map/psum | solution.py:11
  1902.3 19.7 custom-call.28
  1929.6 85.3 %all-reduce.32.cloned.1.call-done = bf16[1792,256]{1,0:T(8,128)(2,1)} async-done(((bf16[1792,256]{1,0:T(8,128)(2,1)}), bf16[1792,256]{1,0:T(8,128)(2,1)}) %all-reduce.32.cloned.1.call-update) | async-done | bytes 917520 | tf_op jit(solution)/shard_map/psum | solution.py:11
  2017.8 137.2 %all-reduce.34.cloned.1.call-done = (bf16[7,1,256,256]{3,2,1,0:T(8,128)(2,1)}, bf16[7,1,256,256]{3,2,1,0:T(8,128)(2,1)}) async-done(((bf16[7,1,256,256]{3,2,1,0:T(8,128)(2,1)}, bf16[7,1,256,256]{3,2,1,0:T(8,128)(2,1)}), (bf16[7,1,256,256]{3,2,1,0:T(8,128)(2,1)}, bf16[7,1,256,256]{3,2,1,0:T(8,128)(2,1)})) %all-reduce.34.cloned.1.call-update) | async-done | bytes 1835024 | tf_op jit(solution)/shard_map/psum | solution.py:11
  2187.9 22.5 %reshape.1094 = bf16[7,1,256,14,1,256]{5,3,2,0,4,1:T(8,128)(2,1)} reshape(bf16[1792,3584]{1,0:T(8,128)(2,1)} %select_convert_fusion) | data formatting | bytes 25690112 | tf_op jit(solution)/shard_map/reshape | solution.py:158
  (288 shorter events, 350.7 us)
Async XLA Ops:
  44.6 11.1 copy-start.4
  44.6 242.4 %all-to-all-start = ((bf16[128,1,1,256,256]{4,3,2,1,0:T(8,128)(2,1)}), bf16[128,1,1,256,256]{4,3,2,1,0:T(8,128)(2,1)}, u32[]{:S(2)}, u32[]{:S(2)}) async-start(bf16[128,1,1,256,256]{4,3,2,1,0:T(8,128)(2,1)} %fusion.2), calls=%async_computation | async-start | bytes 33554432 | tf_op jit(solution)/shard_map/all_to_all | solution.py:109
  55.6 432.5 %all-reduce.18.cloned.1.call-start = ((), (), s32[]{:S(2)}) async-start(), calls=%async_computation.1 | async-start | bytes 524288 | tf_op jit(solution)/shard_map/psum | solution.py:11
  356.3 287.9 %all-reduce.20.cloned.1.call-start = ((), (), s32[]{:S(2)}) async-start(), calls=%async_computation.2 | async-start | bytes 1835008 | tf_op jit(solution)/shard_map/psum | solution.py:11
  554.8 1.2 copy-start.5
  558.9 225.4 %all-reduce.40.cloned.1.call-start = ((), (), s32[]{:S(2)}) async-start(), calls=%async_computation.12 | async-start | bytes 3670016 | tf_op jit(solution)/shard_map/psum | solution.py:11
  646.9 298.8 %all-reduce.22.cloned.1.call-start = ((), (), s32[]{:S(2)}) async-start(), calls=%async_computation.3 | async-start | bytes 524288 | tf_op jit(solution)/shard_map/psum | solution.py:11
  784.4 1.7 copy-start.1
  806.7 294.5 %all-reduce.24.cloned.1.call-start = ((), (), s32[]{:S(2)}) async-start(), calls=%async_computation.4 | async-start | bytes 1835008 | tf_op jit(solution)/shard_map/psum | solution.py:11
  1011.8 1.2 copy-start.6
  1015.9 225.4 %all-reduce.38.cloned.1.call-start = ((), (), s32[]{:S(2)}) async-start(), calls=%async_computation.11 | async-start | bytes 3670016 | tf_op jit(solution)/shard_map/psum | solution.py:11
  1103.8 298.7 %all-reduce.26.cloned.1.call-start = ((), (), s32[]{:S(2)}) async-start(), calls=%async_computation.5 | async-start | bytes 524288 | tf_op jit(solution)/shard_map/psum | solution.py:11
  1241.3 1.7 copy-start.2
  1263.6 294.3 %all-reduce.28.cloned.1.call-start = ((), (), s32[]{:S(2)}) async-start(), calls=%async_computation.6 | async-start | bytes 1835008 | tf_op jit(solution)/shard_map/psum | solution.py:11
  1468.4 1.2 copy-start.7
  1472.6 225.4 %all-reduce.36.cloned.1.call-start = ((), (), s32[]{:S(2)}) async-start(), calls=%async_computation.10 | async-start | bytes 3670016 | tf_op jit(solution)/shard_map/psum | solution.py:11
  1560.5 298.7 %all-reduce.30.cloned.1.call-start = ((), (), s32[]{:S(2)}) async-start(), calls=%async_computation.7 | async-start | bytes 524288 | tf_op jit(solution)/shard_map/psum | solution.py:11
  1698.0 1.7 copy-start.3
  1720.3 294.6 %all-reduce.32.cloned.1.call-start = ((), (), s32[]{:S(2)}) async-start(), calls=%async_computation.8 | async-start | bytes 1835008 | tf_op jit(solution)/shard_map/psum | solution.py:11
  1925.4 1.2 copy-start.8
  1929.6 225.4 %all-reduce.34.cloned.1.call-start = ((), (), s32[]{:S(2)}) async-start(), calls=%async_computation.9 | async-start | bytes 3670016 | tf_op jit(solution)/shard_map/psum | solution.py:11
  2155.0 1.7 copy-start
Sparse Core Ops, SparseCore 0:
  356.5 131.6 all-reduce.17
  559.1 85.1 all-reduce.19
  647.0 137.3 all-reduce.39
  806.8 138.7 all-reduce.21
  1016.1 85.1 all-reduce.23
  1103.9 137.3 all-reduce.37
  1263.8 138.7 all-reduce.25
  1472.7 85.1 all-reduce.27
  1560.6 137.3 all-reduce.35
  1720.5 138.6 all-reduce.29
  1929.7 85.1 all-reduce.31
  2017.6 137.3 all-reduce.33
where the time goes:
time: 2240 us; the launch traced here: 2230 us
  waiting for transfers between devices  1660 us (74%)
  other arithmetic  298 us (13%)
  local copies, waits for them, and re-layouts  137 us (6%)
  matrix products  99.6 us (4%)
    psum x12, waiting for transfers between devices, from_root(): return lax.psum(jnp.where(mine, shard, jnp.zeros_like(shard)), axis)  1440 us
    all_to_all x1, waiting for transfers between devices, per_device(): lax.all_to_all(outgoing, ('row', 'col'), split_axis=0, concat_axis=0, til...  224 us
    another operation x28, other arithmetic, per_device(): factor = jnp.linalg.cholesky(symmetric)  138 us
    another operation x9, other arithmetic, per_device(): jax.scipy.linalg.solve_triangular(factor, jnp.transpose(column), lower=True)  78.8 us
    dot_general x4, matrix products, per_device(): jnp.einsum('ik,jk->ij', panel_low, across, preferred_element_type=jnp.flo...  64.1 us
  transfers between devices with their start and end apart: 13, of which 13 were waited for; matrix products, arithmetic and copies ran while one was open for 0% of the time, Pallas kernels for 0%

commit v1 on v0

v1 whole, which is shorter than its diff:
```python
import functools

import jax
import jax.numpy as jnp
from jax import lax
from jax.experimental import pallas as pl
from jax.experimental.pallas import tpu as pltpu
from jax.sharding import Mesh, PartitionSpec as P

f32 = jnp.float32
bf16 = jnp.bfloat16
i32 = jnp.int32

T = 256
PANELS = 4
NB = 32
RL, CL = 7, 14
K = 7
VMEM = 56 * 1024 * 1024

ROW = ("xh", "y1", "y0", "core")
COL = ("z1", "z0", "xl")
ALL = ROW + COL
PLANE = ("y1", "y0", "core", "z1", "z0")
SPREAD = ("xh", "y1", "z1")
CHIPS = ("xh", "y1", "y0", "z1", "z0", "xl")


def permutation(move):
    pairs = []
    for row in range(16):
        for col in range(8):
            at = (row // 8, row // 2 % 4, row % 2, col // 2, col % 2)
            xh, y, core, z, xl = move(*at)
            pairs.append((row * 8 + col, (xh * 8 + y % 4 * 2 + core) * 8 + z % 4 * 2 + xl))
    return pairs


def exchange(x, axes):
    return lax.all_to_all(x, axes, split_axis=0, concat_axis=0, tiled=True)


def dot_t(a, b):
    return lax.dot_general(a, b, (((1,), (1,)), ((), ())), preferred_element_type=f32)


def split2(x):
    high = x.astype(bf16)
    return high, (x - high.astype(f32)).astype(bf16)


def split3(x):
    high = x.astype(bf16)
    rest = x - high.astype(f32)
    mid = rest.astype(bf16)
    return high, mid, (rest - mid.astype(f32)).astype(bf16)


def solve_t(x, inv_high, inv_low):
    high, low = split2(x)
    return dot_t(high, inv_high) + (dot_t(high, inv_low) + dot_t(low, inv_high))


def pack_kernel(s_ref, x_ref, *out_refs):
    rows = lax.broadcasted_iota(i32, (T, T), 0)
    cols = lax.broadcasted_iota(i32, (T, T), 1)
    pick = jnp.where((rows % 32) * 8 + rows // 32 == cols, 1.0, 0.0).astype(bf16)

    def group(g, _):
        part = x_ref[0, pl.ds(pl.multiple_of(g * T, T), T), :]
        moved = jnp.dot(pick, part, preferred_element_type=f32).astype(bf16)
        at = pl.ds(pl.multiple_of(g * 32, 32), 32)
        for b in range(8):
            for e in range(2):

                @pl.when(s_ref[16 + b] == e)
                def _():
                    out_refs[e][0, s_ref[8 + b], at, :] = moved[b * 32 : (b + 1) * 32]

        return 0

    lax.fori_loop(0, 8, group, 0)


def pack(scalars, tiles):
    shape = jax.ShapeDtypeStruct((8, 4, T, T), bf16)
    spec = pl.BlockSpec((1, 4, T, T), lambda a, s: (s[a], 0, 0, 0))
    return pl.pallas_call(
        pack_kernel,
        out_shape=(shape, shape),
        grid_spec=pltpu.PrefetchScalarGridSpec(
            num_scalar_prefetch=1,
            grid=(8,),
            in_specs=[pl.BlockSpec((1, 8 * T, T), lambda a, s: (a, 0, 0))],
            out_specs=[spec, spec],
        ),
        compiler_params=pltpu.CompilerParams(vmem_limit_bytes=VMEM),
        cost_estimate=pl.CostEstimate(flops=2 * 64 * T**3, bytes_accessed=1 << 24, transcendentals=0),
        name="pack",
    )(scalars, tiles)


def copy_kernel(s_ref, x_ref, out_ref):
    out_ref[...] = x_ref[...]


def compact(which, tiles):
    count = which.shape[0]
    return pl.pallas_call(
        copy_kernel,
        out_shape=jax.ShapeDtypeStruct((count, 4, T, T), bf16),
        grid_spec=pltpu.PrefetchScalarGridSpec(
            num_scalar_prefetch=1,
            grid=(count,),
            in_specs=[pl.BlockSpec((1, 4, T, T), lambda a, s: (s[a], 0, 0, 0))],
            out_specs=pl.BlockSpec((1, 4, T, T), lambda a, s: (a, 0, 0, 0)),
        ),
        compiler_params=pltpu.CompilerParams(vmem_limit_bytes=VMEM),
        cost_estimate=pl.CostEstimate(flops=0, bytes_accessed=count << 20, transcendentals=0),
        name="compact",
    )(which, tiles)


def factor_tile(aug):
    row_id = lax.broadcasted_iota(i32, (8, 128), 0)
    groups = NB // 8

    def block(step, _):
        at = pl.multiple_of(step * NB, NB)
        rows = [aug[pl.ds(pl.multiple_of(at + 8 * g, 8), 8), :] for g in range(groups)]
        back = lax.rem(T - at, T)
        diag = [pltpu.roll(rows[g][:, :T], back, 1)[:, :128] for g in range(groups)]
        scales = []
        for s in range(groups):
            cols = [
                [jnp.broadcast_to(diag[g][:, 8 * s + m : 8 * s + m + 1], (8, 128)) for g in range(s, groups)]
                for m in range(8)
            ]
            scale = jnp.zeros((8, 128), f32)
            for m in range(8):
                pivot = jnp.broadcast_to(cols[m][0][m : m + 1, :], (8, 128))
                inverse = 1.0 / pivot
                scale = jnp.where(row_id == m, lax.rsqrt(pivot), scale)
                factor = [c * inverse for c in cols[m]]
                factor[0] = jnp.where(row_id > m, factor[0], 0.0)
                for later in range(m + 1, 8):
                    value = jnp.broadcast_to(cols[later][0][m : m + 1, :], (8, 128))
                    cols[later] = [c - f * value for c, f in zip(cols[later], factor)]
                diag_row = jnp.broadcast_to(diag[s][m : m + 1, :], (8, 128))
                full_row = rows[s][m : m + 1, :]
                for g in range(s, groups):
                    f = factor[g - s]
                    diag[g] = diag[g] - f * diag_row
                    rows[g] = rows[g] - jnp.concatenate([f] * 4, axis=1) * full_row
            scales.append(scale)
        upper = jnp.concatenate(
            [rows[g] * jnp.concatenate([scales[g]] * 4, axis=1) for g in range(groups)], axis=0
        )
        aug[pl.ds(at, NB), :] = upper
        high, mid, low = split3(upper)
        keep = lax.broadcasted_iota(i32, (NB, T), 1) >= at + NB
        none = jnp.zeros((NB, T), bf16)
        lh, lm, ll = [jnp.where(keep, part[:, :T], none) for part in (high, mid, low)]
        left = jnp.concatenate([lh, lh, lm, lh, ll, lm], axis=0)
        right = jnp.concatenate([high, mid, high, low, high, mid], axis=0)
        aug[...] = aug[...] - lax.dot_general(
            left, right, (((0,), (0,)), ((), ())), preferred_element_type=f32
        )
        return 0

    lax.fori_loop(0, T // NB, block, 0)


def pivot_kernel(core_ref, own_ref, other_ref, shift_ref, lb_ref, high_ref, low_ref, work, aug):
    rows = lax.broadcasted_iota(i32, (T, T), 0)
    cols = lax.broadcasted_iota(i32, (T, T), 1)
    core = core_ref[0]
    for t in range(PANELS):
        for u in range(t + 1):
            for s in range(8):
                at = (((s // 2) * 2 + t // 2) * 2 + s % 2) * 4 + u
                part = jnp.where(core == t % 2, own_ref[at].astype(f32), other_ref[at].astype(f32))
                work[t, u, s * 32 : (s + 1) * 32, :] = part
        tile = jnp.where(rows >= cols, work[t, t], 0.0)
        work[t, t] = tile + jnp.where(rows == cols, 0.0, tile).T + jnp.where(rows == cols, shift_ref[t], 0.0)
    for k in range(PANELS):
        aug[:, :T] = work[k, k]
        aug[:, T:] = jnp.where(rows == cols, 1.0, 0.0)
        factor_tile(aug)
        lower = jnp.where(rows >= cols, aug[:, :T].T, 0.0)
        inv_high, inv_low = split2(aug[:, T:])
        high_ref[k] = inv_high
        low_ref[k] = inv_low
        for t in range(k):
            lb_ref[k, t * T : (t + 1) * T, :] = jnp.zeros((T, T), bf16)
        lb_ref[k, k * T : (k + 1) * T, :] = lower.astype(bf16)
        for t in range(k + 1, PANELS):
            lb_ref[k, t * T : (t + 1) * T, :] = solve_t(work[t, k], inv_high, inv_low).astype(bf16)
        for t in range(k + 1, PANELS):
            for u in range(k + 1, t + 1):
                work[t, u] = work[t, u] - dot_t(
                    lb_ref[k, t * T : (t + 1) * T, :], lb_ref[k, u * T : (u + 1) * T, :]
                )


def pivot(core, own, other, shift):
    vmem = pl.BlockSpec(memory_space=pltpu.VMEM)
    return pl.pallas_call(
        pivot_kernel,
        out_shape=(
            jax.ShapeDtypeStruct((PANELS, PANELS * T, T), bf16),
            jax.ShapeDtypeStruct((PANELS, T, T), bf16),
            jax.ShapeDtypeStruct((PANELS, T, T), bf16),
        ),
        in_specs=[pl.BlockSpec(memory_space=pltpu.SMEM), vmem, vmem, vmem],
        out_specs=[vmem] * 3,
        scratch_shapes=[pltpu.VMEM((PANELS, PANELS, T, T), f32), pltpu.VMEM((T, 2 * T), f32)],
        compiler_params=pltpu.CompilerParams(vmem_limit_bytes=VMEM),
        cost_estimate=pl.CostEstimate(flops=45_000_000_000, bytes_accessed=1 << 22, transcendentals=0),
        name="pivot_factor",
    )(core, own, other, shift)


def panel_kernel(s_ref, strip_ref, coupling_ref, lb_ref, high_ref, low_ref, out_ref):
    a = pl.program_id(0)
    row = s_ref[14]
    found = s_ref[7 + a].astype(f32)
    done = []
    for k in range(PANELS):
        block = strip_ref[:, 0, k].reshape(T, T).astype(f32) * found
        block = block + coupling_ref[0, :, k * T : (k + 1) * T].astype(f32)
        for j in range(k):
            block = block - dot_t(done[j], lb_ref[j, k * T : (k + 1) * T, :])
        solved = solve_t(block, high_ref[k], low_ref[k]).astype(bf16)
        done.append(solved)
        out_ref[0, :, k * T : (k + 1) * T] = solved

    @pl.when((a == 0) & (row < PANELS))
    def _():
        at = pl.ds(pl.multiple_of(row * T, T), T)
        for k in range(PANELS):
            out_ref[0, :, k * T : (k + 1) * T] = lb_ref[k, at, :]


def panel_rows(scalars, strip, coupling, lb, high, low):
    whole = lambda shape: pl.BlockSpec(shape, lambda a, s: (0,) * len(shape))
    return pl.pallas_call(
        panel_kernel,
        out_shape=jax.ShapeDtypeStruct((RL, T, PANELS * T), bf16),
        grid_spec=pltpu.PrefetchScalarGridSpec(
            num_scalar_prefetch=1,
            grid=(RL,),
            in_specs=[
                pl.BlockSpec((8, 1, PANELS, 32, T), lambda a, s: (0, s[a], 0, 0, 0)),
                pl.BlockSpec((1, T, PANELS * T), lambda a, s: (a, 0, 0)),
                whole((PANELS, PANELS * T, T)),
                whole((PANELS, T, T)),
                whole((PANELS, T, T)),
            ],
            out_specs=pl.BlockSpec((1, T, PANELS * T), lambda a, s: (a, 0, 0)),
        ),
        compiler_params=pltpu.CompilerParams(vmem_limit_bytes=VMEM),
        cost_estimate=pl.CostEstimate(flops=8_000_000_000, bytes_accessed=12 << 20, transcendentals=0),
        name="panel_rows",
    )(scalars, strip, coupling, lb, high, low)


PIECES = ((0, 2), (2, 4), (4, 6), (6, 7))


def front_kernel(s_ref, rows_ref, *refs):
    blocks = refs[0:4]
    own, other = refs[4:8], refs[8:12]
    out_ref = refs[12]
    a = pl.program_id(0)
    row, col, core = s_ref[119], s_ref[120], s_ref[121]
    row_ok = [s_ref[21 + a], s_ref[28 + a]]
    mine = rows_ref[0]
    for j, (lo, hi) in enumerate(PIECES):
        for held, parity in ((own[j], core), (other[j], 1 - core)):
            for n in range(hi - lo):
                b = 2 * (lo + n) + parity
                tile = -dot_t(mine, held[n])
                for f in range(2):
                    base = 35 + 42 * f
                    z, e = s_ref[base + b], s_ref[base + 14 + b]
                    ok = row_ok[f] * s_ref[base + 28 + b]
                    at0 = (ok * (1 - e)).astype(f32)
                    at1 = (ok * e).astype(f32)
                    tile = tile + blocks[2 * f][0, z].astype(f32) * at0
                    tile = tile + blocks[2 * f + 1][0, z].astype(f32) * at1
                out_ref[0, b] = tile.astype(bf16)

    @pl.when((a == 0) & (row < PANELS))
    def _():
        out_ref[...] = jnp.zeros_like(out_ref)

    @pl.when(col < PANELS)
    def _():
        out_ref[0, 0] = rows_ref[0, :, pl.ds(pl.multiple_of(jnp.minimum(col, PANELS - 1) * T, T), T)]


def front(scalars, rows, blocks, own, other):
    block = lambda first: pl.BlockSpec((1, 4, T, T), lambda a, s: (s[first + a], 0, 0, 0))
    whole = lambda x: pl.BlockSpec(x.shape, lambda a, s: (0, 0, 0))
    return pl.pallas_call(
        front_kernel,
        out_shape=jax.ShapeDtypeStruct((RL, CL, T, T), bf16),
        grid_spec=pltpu.PrefetchScalarGridSpec(
            num_scalar_prefetch=1,
            grid=(RL,),
            in_specs=[
                pl.BlockSpec((1, T, PANELS * T), lambda a, s: (a, 0, 0)),
                block(0),
                block(7),
                block(14),
                block(14),
            ]
            + [whole(x) for x in own]
            + [whole(x) for x in other],
            out_specs=pl.BlockSpec((1, CL, T, T), lambda a, s: (a, 0, 0, 0)),
        ),
        compiler_params=pltpu.CompilerParams(vmem_limit_bytes=VMEM),
        cost_estimate=pl.CostEstimate(
            flops=2 * RL * CL * T * T * PANELS * T, bytes_accessed=40 << 20, transcendentals=0
        ),
        name="front",
    )(scalars, rows, *blocks, *own, *other)


def per_device(children, child_maps, coupling, pivot_shift):
    row, col = lax.axis_index(ROW), lax.axis_index(COL)
    xh, core, xl = lax.axis_index("xh"), lax.axis_index("core"), lax.axis_index("xl")
    rho = row % 8
    eight = jnp.arange(8)

    own_map = child_maps[xh].reshape(8, 8)
    row_to = jnp.sum(jnp.where(eight[None, :] == rho, own_map, 0), axis=1)
    col_to = jnp.sum(jnp.where(eight[None, :] == col, own_map, 0), axis=1)
    pack_scalars = jnp.concatenate([row_to % 8, col_to % 8 // 2, (col_to % 2) ^ xl]).astype(i32)

    tiles = children.reshape(8, T, 8, T)

    first = tiles[0, :, 0, :].reshape(8, 32, T)
    piece = exchange(first, SPREAD)[0]
    own_half = exchange(jnp.broadcast_to(piece[None], (64, 32, T)), CHIPS)
    swap = permutation(lambda xh, y, core, z, xl: (xh, y, 1 - core, z, xl))
    other_half = lax.ppermute(own_half, ALL, swap)

    sixteen = jnp.arange(16)
    from_a = jnp.sum(jnp.where(row_to[None, :] % 16 == sixteen[:, None], eight[None, :], 0), axis=1)
    strip = tiles[:, :, 0, :].reshape(8, 8, 32, T)[from_a].reshape(128, 32, T)
    strip = exchange(strip, ALL).reshape(16, 8, 32, T)[:8, :PANELS]
    strip = exchange(jnp.broadcast_to(strip[None], (8, 8, PANELS, 32, T)), COL)

    lb, high, low = pivot(core.reshape(1), own_half, other_half, pivot_shift.reshape(PANELS, T, 1))

    both = jnp.stack([child_maps[xh], child_maps[1 - xh]])
    at = jnp.arange(64)
    row_is = both[:, None, :] == (row + 16 * jnp.arange(RL))[None, :, None]
    row_t = jnp.sum(jnp.where(row_is, at, 0), axis=2)
    row_ok = jnp.any(row_is, axis=2).astype(i32)
    col_is = both[:, None, :] == (col + 8 * jnp.arange(CL))[None, :, None]
    col_u = jnp.sum(jnp.where(col_is, at, 0), axis=2)
    col_ok = jnp.any(col_is, axis=2).astype(i32)
    by_q = both.reshape(2, 8, 8)
    half = jnp.sum(jnp.where(by_q % 8 == rho, by_q // 8 % 2, 0), axis=1)
    rank_of = lambda hit: jnp.sum(
        jnp.where(eight[None, :] < eight[:, None], hit[..., None, :].astype(i32), 0), axis=-1
    )
    rank = rank_of(half == xh)
    slot = jnp.sum(jnp.where(row_t[:, :, None] % 8 == eight, rank[:, None, :], 0), axis=2) * row_ok

    def chosen(hit):
        order = jnp.where(hit[None, :] & (rank_of(hit)[None, :] == jnp.arange(K)[:, None]), eight[None, :], 0)
        return jnp.sum(order, axis=1).astype(i32)

    to_own, to_other = chosen(half[0] == xh), chosen(half[0] != xh)

    zero_is = child_maps[0][None, :] == (row + 16 * jnp.arange(RL))[:, None]
    panel_scalars = jnp.concatenate(
        [
            jnp.sum(jnp.where(zero_is, at % 8, 0), axis=1),
            jnp.any(zero_is, axis=1).astype(i32),
            row.reshape(1),
        ]
    ).astype(i32)
    front_scalars = jnp.concatenate(
        [row_t[0] % 8, slot[0], slot[1], row_ok[0], row_ok[1]]
        + [x[f] for f in range(2) for x in (col_u % 8 // 2, (col_u % 2) ^ xl, col_ok)]
        + [row.reshape(1), col.reshape(1), core.reshape(1)]
    ).astype(i32)

    packed_same, packed_cross = pack(pack_scalars, children.reshape(8, 8 * T, T))
    cross = exchange(packed_cross.reshape(32, T, T), PLANE).reshape(8, 4, T, T)
    same = exchange(packed_same.reshape(32, T, T), PLANE).reshape(8, 4, T, T)
    move = lambda f, e: permutation(lambda xh, y, core, z, xl: (xh ^ f, y, core, z, xl ^ e))
    from_01 = lax.ppermute(compact(to_own, cross), ALL, move(0, 1))
    from_11 = lax.ppermute(compact(to_other, cross), ALL, move(1, 1))
    from_10 = lax.ppermute(compact(to_other, same), ALL, move(1, 0))

    rows = panel_rows(panel_scalars, strip, coupling.reshape(RL, T, PANELS * T), lb, high, low)

    own, other = [], []
    for j, (lo, hi) in enumerate(PIECES):
        turn = permutation(lambda xh, y, core, z, xl: (xl ^ (j % 2), z - y + j, xh, y, core))
        own.append(lax.ppermute(rows[lo:hi], ALL, turn))
        other.append(lax.ppermute(own[-1], ALL, swap))

    result = front(front_scalars, rows, (same, from_01, from_10, from_11), own, other)
    return jnp.transpose(result, (0, 2, 1, 3)).reshape(RL, 1, T, CL, 1, T)


def solution(mesh):
    fine = Mesh(mesh.devices.reshape((2,) * 7), ALL)
    in_specs = (P(None, ROW, None, None, COL, None), P(), P(None, ROW, None, None), P())
    out_specs = P(None, ROW, None, None, COL, None)
    return jax.shard_map(per_device, mesh=fine, in_specs=in_specs, out_specs=out_specs, check_vma=False)
```

time: 2240 us -> 471 us (0.21)
  waiting for transfers between devices: 1660 us -> 198 us
  other arithmetic: 298 us -> 4.78 us
  Pallas kernels: 0 us -> 128 us
  local copies, waits for them, and re-layouts: 137 us -> 25.5 us
  matrix products: 99.6 us -> 0 us
  blocking collectives: 0 us -> 55.3 us
  starting transfers between devices: 12.5 us -> 56.4 us
    psum x12 -> x0, waiting for transfers between devices: 1440 us -> none  [from_root(): return lax.psum(jnp.where(mine, shard, jnp.zeros_like(shard)), axis)]
    another operation x44 -> x1, other arithmetic: 225 us -> 0.01 us  [per_device(): both = jnp.stack([child_maps[xh], child_maps[1 - xh]])]
    all_to_all x1 -> x5, waiting for transfers between devices: 224 us -> 90.9 us  [exchange(): return lax.all_to_all(x, axes, split_axis=0, concat_axis=0, tiled=True)]
    pallas_call x0 -> x7, Pallas kernels: none -> 128 us  [the longest x1 42.2 us: pivot(): pl.pallas_call(pivot_kernel, out_shape=(jax.ShapeDtypeStruct((PANELS, PAN...]
    ppermute x0 -> x12, waiting for transfers between devices: none -> 107 us  [the longest x4 102 us: per_device(): own.append(lax.ppermute(rows[lo:hi], ALL, turn))]
    dot_general x5 -> x0, matrix products: 80.3 us -> none  [the longest x4 64.1 us: per_device(): jnp.einsum('ik,jk->ij', panel_low, across, preferred_element_type=jnp.flo...]
    all_to_all x0 -> x1, blocking collectives: none -> 55.3 us  [exchange(): return lax.all_to_all(x, axes, split_axis=0, concat_axis=0, tiled=True)]
    select_n x27 -> x5, other arithmetic: 36.2 us -> 0.05 us  [the longest x1 0.02 us: per_device(): col_to % 8 // 2]
  transfers between devices with their start and end apart: 13 -> 17, of which waited for: 13 -> 11; matrix products, arithmetic and copies ran while one was open for 0% -> 4% of each run, Pallas kernels for 0% -> 21%
where the time goes in v1:
time: 471 us; the launch traced here: 468 us
  waiting for transfers between devices  198 us (42%)
  Pallas kernels  128 us (27%)
  starting transfers between devices  56.4 us (12%)
  blocking collectives  55.3 us (12%)
  local copies, waits for them, and re-layouts  25.5 us (5%)
  other arithmetic  4.78 us (1%)
    ppermute x4, waiting for transfers between devices, per_device(): own.append(lax.ppermute(rows[lo:hi], ALL, turn))  102 us
    all_to_all x5, waiting for transfers between devices, exchange(): return lax.all_to_all(x, axes, split_axis=0, concat_axis=0, tiled=True)  90.9 us
    all_to_all x1, blocking collectives, exchange(): return lax.all_to_all(x, axes, split_axis=0, concat_axis=0, tiled=True)  55.3 us
    pallas_call x1, Pallas kernels, pivot(): pl.pallas_call(pivot_kernel, out_shape=(jax.ShapeDtypeStruct((PANELS, PAN...  42.2 us
    all_to_all x5, starting transfers between devices, exchange(): return lax.all_to_all(x, axes, split_axis=0, concat_axis=0, tiled=True)  32.2 us
    pallas_call x1, Pallas kernels, front(): pl.pallas_call(front_kernel, out_shape=jax.ShapeDtypeStruct((RL, CL, T, T...  28.4 us
    pallas_call x1, Pallas kernels, pack(): pl.pallas_call(pack_kernel, out_shape=(shape, shape), grid_spec=pltpu.Pre...  24.7 us
    pallas_call x3, Pallas kernels, compact(): pl.pallas_call(copy_kernel, out_shape=jax.ShapeDtypeStruct((count, 4, T,...  17.8 us
  transfers between devices with their start and end apart: 17, of which 11 were waited for; matrix products, arithmetic and copies ran while one was open for 4% of the time, Pallas kernels for 21%

profile of v1, /device:TPU:8, one launch (start us, length us, event | category | flops | bytes accessed | tf_op | source)
XLA Modules:
  0.0 467.5 jit_solution(1206111713189670880)
XLA Ops:
  0.0 8.8 %copy.24 = bf16[8,1,256,8,1,256]{5,2,0,3,4,1:T(8,128)(2,1)} copy(bf16[8,1,256,8,1,256]{5,3,4,2,1,0:T(8,128)(2,1)} %param.4) | data formatting | bytes 16777216 | tf_op args[0]
  10.3 9.3 %all-to-all-start.2 = ((bf16[8,32,256]{2,1,0:T(8,128)(2,1)}), bf16[8,32,256]{2,1,0:T(8,128)(2,1)S(1)}, u32[]{:S(2)}, u32[]{:S(2)}) async-start(bf16[8,32,256]{2,1,0:T(8,128)(2,1)} %bitcast.15), calls=%async_computation.2 | async-start | bytes 262144 | tf_op jit(solution)/shard_map/all_to_all | solution.py:40
  19.7 10.6 %all-to-all-done.2 = bf16[8,32,256]{2,1,0:T(8,128)(2,1)S(1)} async-done(((bf16[8,32,256]{2,1,0:T(8,128)(2,1)}), bf16[8,32,256]{2,1,0:T(8,128)(2,1)S(1)}, u32[]{:S(2)}, u32[]{:S(2)}) %all-to-all-start.2) | async-done | bytes 131104 | tf_op jit(solution)/shard_map/all_to_all | solution.py:40
  31.4 6.3 %all-to-all-start.3 = ((bf16[64,32,256]{2,1,0:T(8,128)(2,1)}), bf16[64,32,256]{2,1,0:T(8,128)(2,1)}, u32[]{:S(2)}, u32[]{:S(2)}) async-start(bf16[64,32,256]{2,1,0:T(8,128)(2,1)} %broadcast_in_dim.182), calls=%async_computation.3 | async-start | bytes 2097152 | tf_op jit(solution)/shard_map/all_to_all | solution.py:40
  42.7 11.0 %all-to-all-done.3.own_ref = bf16[64,32,256]{2,1,0:T(8,128)(2,1)} async-done(((bf16[64,32,256]{2,1,0:T(8,128)(2,1)}), bf16[64,32,256]{2,1,0:T(8,128)(2,1)}, u32[]{:S(2)}, u32[]{:S(2)}) %all-to-all-start.3) | async-done | bytes 1048608 | tf_op jit(solution)/shard_map/all_to_all | solution.py:40
  53.6 5.5 %all-to-all-start = ((bf16[128,32,256]{2,1,0:T(8,128)(2,1)}), bf16[128,32,256]{2,1,0:T(8,128)(2,1)S(1)}, u32[]{:S(2)}, u32[]{:S(2)}) async-start(bf16[128,32,256]{2,1,0:T(8,128)(2,1)} %bitcast.12), calls=%async_computation | async-start | bytes 4194304 | tf_op jit(solution)/shard_map/all_to_all | solution.py:40
  59.8 24.7 %pack.1 = (bf16[8,4,256,256]{3,2,1,0:T(8,128)(2,1)}, bf16[8,4,256,256]{3,2,1,0:T(8,128)(2,1)}) custom-call(s32[24]{0:T(128)} %pad_add_fusion.2.s_ref, bf16[8,2048,256]{2,1,0:T(8,128)(2,1)} %bitcast.43), custom_call_target="tpu_custom_call" | custom-call | flops 2147483648 | bytes 16777216 | tf_op jit(solution)/shard_map/pack/pallas_call | solution.py:88
  84.5 4.2 all-to-all-done
  88.7 55.3 %all_to_all.30 = bf16[32,256,256]{2,1,0:T(8,128)(2,1)} all-to-all(bf16[32,256,256]{2,1,0:T(8,128)(2,1)} %bitcast.50), channel_id=1, replica_groups=mesh['xh'=2,'y1'=2,'y0'=2,'core'=2,'z1'=2,'z0'=2,'xl'=2] {'y1','y0','cor..., dimensions={0} | all-to-all | bytes 8388608 | tf_op jit(solution)/shard_map/all_to_all | solution.py:40
  144.1 6.4 %all-to-all-start.5 = ((bf16[32,256,256]{2,1,0:T(8,128)(2,1)}), bf16[32,256,256]{2,1,0:T(8,128)(2,1)}, u32[]{:S(2)}, u32[]{:S(2)}) async-start(bf16[32,256,256]{2,1,0:T(8,128)(2,1)} %bitcast.49), calls=%async_computation.5 | async-start | bytes 8388608 | tf_op jit(solution)/shard_map/all_to_all | solution.py:40
  154.6 5.7 %compact.4 = bf16[7,4,256,256]{3,2,1,0:T(8,128)(2,1)} custom-call(s32[7]{0:T(128)} %select_reduce_fusion.1.s_ref, bf16[8,4,256,256]{3,2,1,0:T(8,128)(2,1)} %bitcast.44), custom_call_target="tpu_custom_call" | custom-call | bytes 7340032 | tf_op jit(solution)/shard_map/compact/pallas_call | solution.py:109
  161.6 39.4 %all-to-all-done.5 = bf16[32,256,256]{2,1,0:T(8,128)(2,1)} async-done(((bf16[32,256,256]{2,1,0:T(8,128)(2,1)}), bf16[32,256,256]{2,1,0:T(8,128)(2,1)}, u32[]{:S(2)}, u32[]{:S(2)}) %all-to-all-start.5) | async-done | bytes 4194336 | tf_op jit(solution)/shard_map/all_to_all | solution.py:40
  203.5 4.8 %all-to-all-start.1 = ((bf16[8,8,4,32,256]{4,3,2,1,0:T(8,128)(2,1)}), bf16[8,8,4,32,256]{4,3,2,1,0:T(8,128)(2,1)}, u32[]{:S(2)}, u32[]{:S(2)}) async-start(bf16[8,8,4,32,256]{4,3,2,1,0:T(8,128)(2,1)} %broadcast_in_dim.180), calls=%async_computation.1 | async-start | bytes 8388608 | tf_op jit(solution)/shard_map/all_to_all | solution.py:40
  208.3 42.2 %pivot_factor.1 = (bf16[4,1024,256]{2,1,0:T(8,128)(2,1)}, bf16[4,256,256]{2,1,0:T(8,128)(2,1)}, bf16[4,256,256]{2,1,0:T(8,128)(2,1)}) custom-call(s32[1]{0:T(128)} %bitcast.6.core_ref, bf16[64,32,256]{2,1,0:T(8,128)(2,1)} %all-to-all-done.3.own_ref, bf16[64,32,256]{2,1,0:T(8,128)(2,1)} %collective-permute-done.other_ref, f32[4,256,1]{2,1,0:T(8,128)} %reshape.166.shift_ref), custom_call_target="tpu_custom_call" | custom-call | flops 44999999488 | bytes 4194304 | tf_op jit(solution)/shard_map/pivot_factor/pallas_call | solution.py:208
  250.5 5.8 %compact.5 = bf16[7,4,256,256]{3,2,1,0:T(8,128)(2,1)} custom-call(s32[7]{0:T(128)} %select_reduce_fusion.1.s_ref, bf16[8,4,256,256]{3,2,1,0:T(8,128)(2,1)} %bitcast.22.x_ref), custom_call_target="tpu_custom_call" | custom-call | bytes 7340032 | tf_op jit(solution)/shard_map/compact/pallas_call | solution.py:109
  256.3 6.2 %compact.3 = bf16[7,4,256,256]{3,2,1,0:T(8,128)(2,1)} custom-call(s32[7]{0:T(128)} %select_reduce_fusion.3.s_ref, bf16[8,4,256,256]{3,2,1,0:T(8,128)(2,1)} %bitcast.22.x_ref), custom_call_target="tpu_custom_call" | custom-call | bytes 7340032 | tf_op jit(solution)/shard_map/compact/pallas_call | solution.py:109
  264.5 25.7 %all-to-all-done.1.strip_ref = bf16[8,8,4,32,256]{4,3,2,1,0:T(8,128)(2,1)} async-done(((bf16[8,8,4,32,256]{4,3,2,1,0:T(8,128)(2,1)}), bf16[8,8,4,32,256]{4,3,2,1,0:T(8,128)(2,1)}, u32[]{:S(2)}, u32[]{:S(2)}) %all-to-all-start.1) | async-done | bytes 4194336 | tf_op jit(solution)/shard_map/all_to_all | solution.py:40
  290.3 14.6 %panel_rows.1.rows_ref = bf16[7,256,1024]{2,1,0:T(8,128)(2,1)} custom-call(s32[15]{0:T(128)} %pad_add_fusion.1.s_ref, bf16[8,8,4,32,256]{4,3,2,1,0:T(8,128)(2,1)} %all-to-all-done.1.strip_ref, bf16[7,256,1024]{2,1,0:T(8,128)(2,1)} %bitcast.52, bf16[4,1024,256]{2,1,0:T(8,128)(2,1)} %get-tuple-element.10.lb_ref, ...), custom_call_target="tpu_custom_call" | custom-call | flops 8000000000 | bytes 12582912 | tf_op jit(solution)/shard_map/panel_rows/pallas_call | solution.py:247
  314.3 66.6 %collective-permute-done.7.refs_7_ = bf16[1,256,1024]{2,1,0:T(8,128)(2,1)S(1)} collective-permute-done((bf16[1,256,1024]{2,1,0:T(8,128)(2,1)S(1)}, bf16[1,256,1024]{2,1,0:T(8,128)(2,1)S(1)}, u32[]{:S(2)}, u32[]{:S(2)}) %collective-permute-start.7) | collective-permute-done | bytes 524320 | tf_op jit(solution)/shard_map/ppermute | solution.py:407
  384.9 3.8 collective-permute-start.4
  389.9 21.3 %collective-permute-done.5.refs_5_ = bf16[2,256,1024]{2,1,0:T(8,128)(2,1)} collective-permute-done((bf16[2,256,1024]{2,1,0:T(8,128)(2,1)S(1)}, bf16[2,256,1024]{2,1,0:T(8,128)(2,1)}, u32[]{:S(2)}, u32[]{:S(2)}) %collective-permute-start.5) | collective-permute-done | bytes 1048608 | tf_op jit(solution)/shard_map/ppermute | solution.py:407
  411.3 8.1 %collective-permute-start.10 = (bf16[2,256,1024]{2,1,0:T(8,128)(2,1)}, bf16[2,256,1024]{2,1,0:T(8,128)(2,1)S(1)}, u32[]{:S(2)}, u32[]{:S(2)}) collective-permute-start(bf16[2,256,1024]{2,1,0:T(8,128)(2,1)} %copy-done.2), channel_id=1, source_target_pairs={{0,8},{1,9},{2,10},{3,11},{4,12},{5,13},{6,14},{7,15},{8,0},{9,1},... | collective-permute-start | bytes 3145736 | tf_op jit(solution)/shard_map/ppermute | solution.py:408
  419.4 14.4 %collective-permute-done.4.refs_4_ = bf16[2,256,1024]{2,1,0:T(8,128)(2,1)} collective-permute-done((bf16[2,256,1024]{2,1,0:T(8,128)(2,1)S(1)}, bf16[2,256,1024]{2,1,0:T(8,128)(2,1)}, u32[]{:S(2)}, u32[]{:S(2)}) %collective-permute-start.4) | collective-permute-done | bytes 1048608 | tf_op jit(solution)/shard_map/ppermute | solution.py:407
  439.2 28.4 %front.1 = bf16[7,14,256,256]{3,2,1,0:T(8,128)(2,1)} custom-call(s32[122]{0:T(128)} %concatenate.9.s_ref, bf16[7,256,1024]{2,1,0:T(8,128)(2,1)} %panel_rows.1.rows_ref, bf16[8,4,256,256]{3,2,1,0:T(8,128)(2,1)} %bitcast.45, bf16[7,4,256,256]{3,2,1,0:T(8,128)(2,1)} %collective-permute-done.1.refs_1_, bf16[7,4,256,256]{3,2,1,0:T(8,128)(2,1)} %collective-permute-done.2.refs_2_, ...), custom_call_target="tpu_custom_call" | custom-call | flops 13153337344 | bytes 41943040 | tf_op jit(solution)/shard_map/front/pallas_call | solution.py:306
  (92 shorter events, 38.1 us)
Async XLA Ops:
  8.8 29.5 %copy-start.1 = (s32[2,64]{1,0:T(2,128)S(1)}, s32[2,64]{1,0:T(2,128)}, u32[]{:S(2)}) copy-start(s32[2,64]{1,0:T(2,128)} %param.5) | copy-start | bytes 1540
  10.3 20.0 %all-to-all-start.2 = ((bf16[8,32,256]{2,1,0:T(8,128)(2,1)}), bf16[8,32,256]{2,1,0:T(8,128)(2,1)S(1)}, u32[]{:S(2)}, u32[]{:S(2)}) async-start(bf16[8,32,256]{2,1,0:T(8,128)(2,1)} %bitcast.15), calls=%async_computation.2 | async-start | bytes 262144 | tf_op jit(solution)/shard_map/all_to_all | solution.py:40
  31.4 22.2 %all-to-all-start.3 = ((bf16[64,32,256]{2,1,0:T(8,128)(2,1)}), bf16[64,32,256]{2,1,0:T(8,128)(2,1)}, u32[]{:S(2)}, u32[]{:S(2)}) async-start(bf16[64,32,256]{2,1,0:T(8,128)(2,1)} %broadcast_in_dim.182), calls=%async_computation.3 | async-start | bytes 2097152 | tf_op jit(solution)/shard_map/all_to_all | solution.py:40
  53.6 35.1 %all-to-all-start = ((bf16[128,32,256]{2,1,0:T(8,128)(2,1)}), bf16[128,32,256]{2,1,0:T(8,128)(2,1)S(1)}, u32[]{:S(2)}, u32[]{:S(2)}) async-start(bf16[128,32,256]{2,1,0:T(8,128)(2,1)} %bitcast.12), calls=%async_computation | async-start | bytes 4194304 | tf_op jit(solution)/shard_map/all_to_all | solution.py:40
  144.0 6.9 %copy-start = (f32[1024]{0:T(1024)S(1)}, f32[1024]{0:T(1024)}, u32[]{:S(2)}) copy-start(f32[1024]{0:T(1024)} %param.7) | copy-start | bytes 12292
  144.1 56.9 %all-to-all-start.5 = ((bf16[32,256,256]{2,1,0:T(8,128)(2,1)}), bf16[32,256,256]{2,1,0:T(8,128)(2,1)}, u32[]{:S(2)}, u32[]{:S(2)}) async-start(bf16[32,256,256]{2,1,0:T(8,128)(2,1)} %bitcast.49), calls=%async_computation.5 | async-start | bytes 8388608 | tf_op jit(solution)/shard_map/all_to_all | solution.py:40
  150.7 57.6 %collective-permute-start = (bf16[64,32,256]{2,1,0:T(8,128)(2,1)}, bf16[64,32,256]{2,1,0:T(8,128)(2,1)}, u32[]{:S(2)}, u32[]{:S(2)}) collective-permute-start(bf16[64,32,256]{2,1,0:T(8,128)(2,1)} %all-to-all-done.3.own_ref), channel_id=1, source_target_pairs={{0,8},{1,9},{2,10},{3,11},{4,12},{5,13},{6,14},{7,15},{8,0},{9,1},... | collective-permute-start | bytes 3145736 | tf_op jit(solution)/shard_map/ppermute | solution.py:348
  160.3 273.5 %collective-permute-start.2 = (bf16[7,4,256,256]{3,2,1,0:T(8,128)(2,1)}, bf16[7,4,256,256]{3,2,1,0:T(8,128)(2,1)}, u32[]{:S(2)}, u32[]{:S(2)}) collective-permute-start(bf16[7,4,256,256]{3,2,1,0:T(8,128)(2,1)} %compact.4), channel_id=1, source_target_pairs={{0,64},{1,65},{2,66},{3,67},{4,68},{5,69},{6,70},{7,71},{8,72},{9,... | collective-permute-start | bytes 11010056 | tf_op jit(solution)/shard_map/ppermute | solution.py:400
  203.5 86.8 %all-to-all-start.1 = ((bf16[8,8,4,32,256]{4,3,2,1,0:T(8,128)(2,1)}), bf16[8,8,4,32,256]{4,3,2,1,0:T(8,128)(2,1)}, u32[]{:S(2)}, u32[]{:S(2)}) async-start(bf16[8,8,4,32,256]{4,3,2,1,0:T(8,128)(2,1)} %broadcast_in_dim.180), calls=%async_computation.1 | async-start | bytes 8388608 | tf_op jit(solution)/shard_map/all_to_all | solution.py:40
  262.5 173.0 %collective-permute-start.3 = (bf16[7,4,256,256]{3,2,1,0:T(8,128)(2,1)}, bf16[7,4,256,256]{3,2,1,0:T(8,128)(2,1)}, u32[]{:S(2)}, u32[]{:S(2)}) collective-permute-start(bf16[7,4,256,256]{3,2,1,0:T(8,128)(2,1)} %compact.5), channel_id=1, source_target_pairs={{0,65},{1,64},{2,67},{3,66},{4,69},{5,68},{6,71},{7,70},{8,73},{9,... | collective-permute-start | bytes 11010056 | tf_op jit(solution)/shard_map/ppermute | solution.py:399
  264.5 171.0 %collective-permute-start.1 = (bf16[7,4,256,256]{3,2,1,0:T(8,128)(2,1)}, bf16[7,4,256,256]{3,2,1,0:T(8,128)(2,1)}, u32[]{:S(2)}, u32[]{:S(2)}) collective-permute-start(bf16[7,4,256,256]{3,2,1,0:T(8,128)(2,1)} %compact.3), channel_id=1, source_target_pairs={{0,1},{1,0},{2,3},{3,2},{4,5},{5,4},{6,7},{7,6},{8,9},{9,8},{10,11... | collective-permute-start | bytes 11010056 | tf_op jit(solution)/shard_map/ppermute | solution.py:398
  306.0 74.9 %collective-permute-start.7 = (bf16[1,256,1024]{2,1,0:T(8,128)(2,1)S(1)}, bf16[1,256,1024]{2,1,0:T(8,128)(2,1)S(1)}, u32[]{:S(2)}, u32[]{:S(2)}) collective-permute-start(bf16[1,256,1024]{2,1,0:T(8,128)(2,1)S(1)} %slice.98), channel_id=1, source_target_pairs={{0,112},{1,48},{2,64},{3,0},{4,80},{5,16},{6,96},{7,32},{8,113},{9... | collective-permute-start | bytes 1572872 | tf_op jit(solution)/shard_map/ppermute | solution.py:407
  311.2 73.7 %collective-permute-start.6 = (bf16[2,256,1024]{2,1,0:T(8,128)(2,1)S(1)}, bf16[2,256,1024]{2,1,0:T(8,128)(2,1)S(1)}, u32[]{:S(2)}, u32[]{:S(2)}) collective-permute-start(bf16[2,256,1024]{2,1,0:T(8,128)(2,1)S(1)} %get-tuple-element.29), channel_id=1, source_target_pairs={{0,32},{1,96},{2,48},{3,112},{4,0},{5,64},{6,16},{7,80},{8,33},{9,... | collective-permute-start | bytes 3145736 | tf_op jit(solution)/shard_map/ppermute | solution.py:407
  380.9 7.8 %copy-start.5 = (bf16[1,256,1024]{2,1,0:T(8,128)(2,1)}, bf16[1,256,1024]{2,1,0:T(8,128)(2,1)S(1)}, u32[]{:S(2)}) copy-start(bf16[1,256,1024]{2,1,0:T(8,128)(2,1)S(1)} %collective-permute-done.7.refs_7_) | copy-start | bytes 1572868
  380.9 1.9 collective-permute-start.11
  382.8 5.9 %copy-start.6 = (bf16[1,256,1024]{2,1,0:T(8,128)(2,1)}, bf16[1,256,1024]{2,1,0:T(8,128)(2,1)S(1)}, u32[]{:S(2)}) copy-start(bf16[1,256,1024]{2,1,0:T(8,128)(2,1)S(1)} %collective-permute-done.11.refs_11_) | copy-start | bytes 1572868
  382.8 28.5 %collective-permute-start.5 = (bf16[2,256,1024]{2,1,0:T(8,128)(2,1)S(1)}, bf16[2,256,1024]{2,1,0:T(8,128)(2,1)}, u32[]{:S(2)}, u32[]{:S(2)}) collective-permute-start(bf16[2,256,1024]{2,1,0:T(8,128)(2,1)S(1)} %get-tuple-element.30), channel_id=1, source_target_pairs={{0,80},{1,16},{2,96},{3,32},{4,112},{5,48},{6,64},{7,0},{8,81},{9,... | collective-permute-start | bytes 3145736 | tf_op jit(solution)/shard_map/ppermute | solution.py:407
  384.9 3.8 copy-start.2
  384.9 48.9 %collective-permute-start.4 = (bf16[2,256,1024]{2,1,0:T(8,128)(2,1)S(1)}, bf16[2,256,1024]{2,1,0:T(8,128)(2,1)}, u32[]{:S(2)}, u32[]{:S(2)}) collective-permute-start(bf16[2,256,1024]{2,1,0:T(8,128)(2,1)S(1)} %get-tuple-element.31), channel_id=1, source_target_pairs={{0,0},{1,64},{2,16},{3,80},{4,32},{5,96},{6,48},{7,112},{8,1},{9,6... | collective-permute-start | bytes 3145736 | tf_op jit(solution)/shard_map/ppermute | solution.py:407
  411.3 24.2 %collective-permute-start.10 = (bf16[2,256,1024]{2,1,0:T(8,128)(2,1)}, bf16[2,256,1024]{2,1,0:T(8,128)(2,1)S(1)}, u32[]{:S(2)}, u32[]{:S(2)}) collective-permute-start(bf16[2,256,1024]{2,1,0:T(8,128)(2,1)} %copy-done.2), channel_id=1, source_target_pairs={{0,8},{1,9},{2,10},{3,11},{4,12},{5,13},{6,14},{7,15},{8,0},{9,1},... | collective-permute-start | bytes 3145736 | tf_op jit(solution)/shard_map/ppermute | solution.py:408
  433.8 4.3 collective-permute-start.9
  433.8 4.5 collective-permute-start.8
  435.5 2.8 copy-start.3
  438.1 1.0 copy-start.4

commit v2 on v1

--- a/solution.py
+++ b/solution.py
@@ -1,5 +1,3 @@
-import functools
-
 import jax
 import jax.numpy as jnp
 from jax import lax
@@ -16,13 +14,13 @@
 NB = 32
 RL, CL = 7, 14
 K = 7
+FIRST = 5
 VMEM = 56 * 1024 * 1024
 
 ROW = ("xh", "y1", "y0", "core")
 COL = ("z1", "z0", "xl")
 ALL = ROW + COL
 PLANE = ("y1", "y0", "core", "z1", "z0")
-SPREAD = ("xh", "y1", "z1")
 CHIPS = ("xh", "y1", "y0", "z1", "z0", "xl")
 
 
@@ -61,25 +59,23 @@
     return dot_t(high, inv_high) + (dot_t(high, inv_low) + dot_t(low, inv_high))
 
 
-def pack_kernel(s_ref, x_ref, *out_refs):
+def pack_kernel(s_ref, x_ref, same_ref, cross_ref, strip_ref, first_ref, moved):
     rows = lax.broadcasted_iota(i32, (T, T), 0)
     cols = lax.broadcasted_iota(i32, (T, T), 1)
     pick = jnp.where((rows % 32) * 8 + rows // 32 == cols, 1.0, 0.0).astype(bf16)
-
-    def group(g, _):
-        part = x_ref[0, pl.ds(pl.multiple_of(g * T, T), T), :]
-        moved = jnp.dot(pick, part, preferred_element_type=f32).astype(bf16)
-        at = pl.ds(pl.multiple_of(g * 32, 32), 32)
-        for b in range(8):
-            for e in range(2):
-
-                @pl.when(s_ref[16 + b] == e)
-                def _():
-                    out_refs[e][0, s_ref[8 + b], at, :] = moved[b * 32 : (b + 1) * 32]
-
-        return 0
-
-    lax.fori_loop(0, 8, group, 0)
+    for g in range(8):
+        part = x_ref[0, g * T : (g + 1) * T, :]
+        tiles = jnp.dot(pick, part, preferred_element_type=f32).astype(bf16)
+        moved[g % 2] = tiles
+        strip_ref[0, g] = tiles[:32]
+        for e, out_ref in enumerate((same_ref, cross_ref)):
+            for z in range(4):
+                at = pl.ds(pl.multiple_of(s_ref[16 + 4 * e + z] * 32, 32), 32)
+                out_ref[0, z, g * 32 : (g + 1) * 32, :] = moved[g % 2, at, :]
+
+    @pl.when(pl.program_id(0) == 0)
+    def _():
+        first_ref[...] = strip_ref[0]
 
 
 def pack(scalars, tiles):
@@ -87,12 +83,23 @@
     spec = pl.BlockSpec((1, 4, T, T), lambda a, s: (s[a], 0, 0, 0))
     return pl.pallas_call(
         pack_kernel,
-        out_shape=(shape, shape),
+        out_shape=(
+            shape,
+            shape,
+            jax.ShapeDtypeStruct((16, 8, 32, T), bf16),
+            jax.ShapeDtypeStruct((8, 32, T), bf16),
+        ),
         grid_spec=pltpu.PrefetchScalarGridSpec(
             num_scalar_prefetch=1,
             grid=(8,),
             in_specs=[pl.BlockSpec((1, 8 * T, T), lambda a, s: (a, 0, 0))],
-            out_specs=[spec, spec],
+            out_specs=[
+                spec,
+                spec,
+                pl.BlockSpec((1, 8, 32, T), lambda a, s: (s[8 + a], 0, 0, 0)),
+                pl.BlockSpec((8, 32, T), lambda a, s: (0, 0, 0)),
+            ],
+            scratch_shapes=[pltpu.VMEM((2, T, T), bf16)],
         ),
         compiler_params=pltpu.CompilerParams(vmem_limit_bytes=VMEM),
         cost_estimate=pl.CostEstimate(flops=2 * 64 * T**3, bytes_accessed=1 << 24, transcendentals=0),
@@ -100,25 +107,28 @@
     )(scalars, tiles)
 
 
-def copy_kernel(s_ref, x_ref, out_ref):
-    out_ref[...] = x_ref[...]
-
-
-def compact(which, tiles):
-    count = which.shape[0]
+def copy_kernel(s_ref, *refs):
+    half = len(refs) // 2
+    for x_ref, out_ref in zip(refs[:half], refs[half:]):
+        out_ref[...] = x_ref[...]
+
+
+def compact(lists, tiles):
+    count = lists[0].shape[0]
+    block = lambda n: pl.BlockSpec((1, 4, T, T), lambda a, s: (s[n * count + a], 0, 0, 0))
     return pl.pallas_call(
         copy_kernel,
-        out_shape=jax.ShapeDtypeStruct((count, 4, T, T), bf16),
+        out_shape=[jax.ShapeDtypeStruct((count, 4, T, T), bf16) for _ in lists],
         grid_spec=pltpu.PrefetchScalarGridSpec(
             num_scalar_prefetch=1,
             grid=(count,),
-            in_specs=[pl.BlockSpec((1, 4, T, T), lambda a, s: (s[a], 0, 0, 0))],
-            out_specs=pl.BlockSpec((1, 4, T, T), lambda a, s: (a, 0, 0, 0)),
+            in_specs=[block(n) for n in range(len(lists))],
+            out_specs=[pl.BlockSpec((1, 4, T, T), lambda a, s: (a, 0, 0, 0)) for _ in lists],
         ),
         compiler_params=pltpu.CompilerParams(vmem_limit_bytes=VMEM),
-        cost_estimate=pl.CostEstimate(flops=0, bytes_accessed=count << 20, transcendentals=0),
+        cost_estimate=pl.CostEstimate(flops=0, bytes_accessed=len(lists) * count << 20, transcendentals=0),
         name="compact",
-    )(which, tiles)
+    )(jnp.concatenate(lists), *[tiles for _ in lists])
 
 
 def factor_tile(aug):
@@ -221,57 +231,69 @@
     )(core, own, other, shift)
 
 
-def panel_kernel(s_ref, strip_ref, coupling_ref, lb_ref, high_ref, low_ref, out_ref):
-    a = pl.program_id(0)
-    row = s_ref[14]
-    found = s_ref[7 + a].astype(f32)
-    done = []
-    for k in range(PANELS):
-        block = strip_ref[:, 0, k].reshape(T, T).astype(f32) * found
-        block = block + coupling_ref[0, :, k * T : (k + 1) * T].astype(f32)
-        for j in range(k):
-            block = block - dot_t(done[j], lb_ref[j, k * T : (k + 1) * T, :])
-        solved = solve_t(block, high_ref[k], low_ref[k]).astype(bf16)
-        done.append(solved)
-        out_ref[0, :, k * T : (k + 1) * T] = solved
-
-    @pl.when((a == 0) & (row < PANELS))
+PIECES = ((0, 4), (4, 7))
+
+
+def panel_kernel(s_ref, *refs):
+    strips, (coupling_ref, lb_ref, high_ref, low_ref) = refs[:2], refs[2:6]
+    *outs, all_ref, done, block = refs[6:]
+    k = pl.program_id(0)
+    row, col = s_ref[14], s_ref[15]
+    for a in range(RL):
+        q = s_ref[a]
+        for d in range(8):
+            at = pl.ds(pl.multiple_of(a * T + (col ^ d) * 32, 32), 32)
+            held = jnp.where(s_ref[7 + a] == 1, strips[d % 2][d // 2, q, 0].astype(f32), 0.0)
+            block[at, :] = held
+        at = slice(a * T, (a + 1) * T)
+        block[at, :] = block[at, :] + coupling_ref[a].astype(f32)
+    for j in range(PANELS - 1):
+
+        @pl.when(j < k)
+        def _():
+            block[...] = block[...] - dot_t(done[j], lb_ref[j, pl.ds(pl.multiple_of(k * T, T), T), :])
+
+    solved = solve_t(block[...], high_ref[k], low_ref[k]).astype(bf16)
+    done[k] = solved
+    all_ref[...] = solved.reshape(RL, T, T)
+    for j, (lo, hi) in enumerate(PIECES):
+        outs[j][...] = solved[lo * T : hi * T].reshape(hi - lo, T, T)
+
+    @pl.when(row < PANELS)
     def _():
-        at = pl.ds(pl.multiple_of(row * T, T), T)
-        for k in range(PANELS):
-            out_ref[0, :, k * T : (k + 1) * T] = lb_ref[k, at, :]
-
-
-def panel_rows(scalars, strip, coupling, lb, high, low):
-    whole = lambda shape: pl.BlockSpec(shape, lambda a, s: (0,) * len(shape))
+        pivot_rows = lb_ref[k, pl.ds(pl.multiple_of(jnp.minimum(row, PANELS - 1) * T, T), T), :]
+        outs[0][0] = pivot_rows
+        all_ref[0] = pivot_rows
+
+
+def panel_rows(scalars, strips, coupling, lb, high, low):
+    whole = lambda shape: pl.BlockSpec(shape, lambda k, s: (0,) * len(shape))
     return pl.pallas_call(
         panel_kernel,
-        out_shape=jax.ShapeDtypeStruct((RL, T, PANELS * T), bf16),
+        out_shape=[jax.ShapeDtypeStruct((hi - lo, T, PANELS * T), bf16) for lo, hi in (*PIECES, (0, RL))],
         grid_spec=pltpu.PrefetchScalarGridSpec(
             num_scalar_prefetch=1,
-            grid=(RL,),
-            in_specs=[
-                pl.BlockSpec((8, 1, PANELS, 32, T), lambda a, s: (0, s[a], 0, 0, 0)),
-                pl.BlockSpec((1, T, PANELS * T), lambda a, s: (a, 0, 0)),
+            grid=(PANELS,),
+            in_specs=[pl.BlockSpec((4, 8, 1, 32, T), lambda k, s: (0, 0, k, 0, 0))] * 2
+            + [
+                pl.BlockSpec((RL, T, T), lambda k, s: (0, 0, k)),
                 whole((PANELS, PANELS * T, T)),
                 whole((PANELS, T, T)),
                 whole((PANELS, T, T)),
             ],
-            out_specs=pl.BlockSpec((1, T, PANELS * T), lambda a, s: (a, 0, 0)),
+            out_specs=[pl.BlockSpec((hi - lo, T, T), lambda k, s: (0, 0, k)) for lo, hi in (*PIECES, (0, RL))],
+            scratch_shapes=[pltpu.VMEM((PANELS, RL * T, T), bf16), pltpu.VMEM((RL * T, T), f32)],
         ),
         compiler_params=pltpu.CompilerParams(vmem_limit_bytes=VMEM),
         cost_estimate=pl.CostEstimate(flops=8_000_000_000, bytes_accessed=12 << 20, transcendentals=0),
         name="panel_rows",
-    )(scalars, strip, coupling, lb, high, low)
-
-
-PIECES = ((0, 2), (2, 4), (4, 6), (6, 7))
+    )(scalars, *strips, coupling, lb, high, low)
 
 
 def front_kernel(s_ref, rows_ref, *refs):
     blocks = refs[0:4]
-    own, other = refs[4:8], refs[8:12]
-    out_ref = refs[12]
+    count = len(PIECES)
+    own, other, out_ref = refs[4 : 4 + count], refs[4 + count : 4 + 2 * count], refs[-1]
     a = pl.program_id(0)
     row, col, core = s_ref[119], s_ref[120], s_ref[121]
     row_ok = [s_ref[21 + a], s_ref[28 + a]]
@@ -285,10 +307,8 @@
                     base = 35 + 42 * f
                     z, e = s_ref[base + b], s_ref[base + 14 + b]
                     ok = row_ok[f] * s_ref[base + 28 + b]
-                    at0 = (ok * (1 - e)).astype(f32)
-                    at1 = (ok * e).astype(f32)
-                    tile = tile + blocks[2 * f][0, z].astype(f32) * at0
-                    tile = tile + blocks[2 * f + 1][0, z].astype(f32) * at1
+                    near, far = blocks[2 * f][0, z].astype(f32), blocks[2 * f + 1][0, z].astype(f32)
+                    tile = tile + jnp.where(e == 0, near, far) * ok.astype(f32)
                 out_ref[0, b] = tile.astype(bf16)
 
     @pl.when((a == 0) & (row < PANELS))
@@ -337,23 +357,11 @@
     own_map = child_maps[xh].reshape(8, 8)
     row_to = jnp.sum(jnp.where(eight[None, :] == rho, own_map, 0), axis=1)
     col_to = jnp.sum(jnp.where(eight[None, :] == col, own_map, 0), axis=1)
-    pack_scalars = jnp.concatenate([row_to % 8, col_to % 8 // 2, (col_to % 2) ^ xl]).astype(i32)
-
-    tiles = children.reshape(8, T, 8, T)
-
-    first = tiles[0, :, 0, :].reshape(8, 32, T)
-    piece = exchange(first, SPREAD)[0]
-    own_half = exchange(jnp.broadcast_to(piece[None], (64, 32, T)), CHIPS)
-    swap = permutation(lambda xh, y, core, z, xl: (xh, y, 1 - core, z, xl))
-    other_half = lax.ppermute(own_half, ALL, swap)
-
-    sixteen = jnp.arange(16)
-    from_a = jnp.sum(jnp.where(row_to[None, :] % 16 == sixteen[:, None], eight[None, :], 0), axis=1)
-    strip = tiles[:, :, 0, :].reshape(8, 8, 32, T)[from_a].reshape(128, 32, T)
-    strip = exchange(strip, ALL).reshape(16, 8, 32, T)[:8, :PANELS]
-    strip = exchange(jnp.broadcast_to(strip[None], (8, 8, PANELS, 32, T)), COL)
-
-    lb, high, low = pivot(core.reshape(1), own_half, other_half, pivot_shift.reshape(PANELS, T, 1))
+    by_to = lambda slots: jnp.sum(jnp.where(col_to[None, :] % 8 == slots[:, None], eight[None, :], 0), axis=1)
+    same_to = 2 * jnp.arange(4) + xl
+    pack_scalars = jnp.concatenate(
+        [row_to % 8, row_to % 16, by_to(same_to), by_to(same_to ^ 1)]
+    ).astype(i32)
 
     both = jnp.stack([child_maps[xh], child_maps[1 - xh]])
     at = jnp.arange(64)
@@ -383,6 +391,7 @@
             jnp.sum(jnp.where(zero_is, at % 8, 0), axis=1),
             jnp.any(zero_is, axis=1).astype(i32),
             row.reshape(1),
+            col.reshape(1),
         ]
     ).astype(i32)
     front_scalars = jnp.concatenate(
@@ -391,23 +400,68 @@
         + [row.reshape(1), col.reshape(1), core.reshape(1)]
     ).astype(i32)
 
-    packed_same, packed_cross = pack(pack_scalars, children.reshape(8, 8 * T, T))
-    cross = exchange(packed_cross.reshape(32, T, T), PLANE).reshape(8, 4, T, T)
-    same = exchange(packed_same.reshape(32, T, T), PLANE).reshape(8, 4, T, T)
+    tiles = children.reshape(8, 8 * T, T)
+    same, cross, strip, first = pack(pack_scalars, tiles)
+
     move = lambda f, e: permutation(lambda xh, y, core, z, xl: (xh ^ f, y, core, z, xl ^ e))
-    from_01 = lax.ppermute(compact(to_own, cross), ALL, move(0, 1))
-    from_11 = lax.ppermute(compact(to_other, cross), ALL, move(1, 1))
-    from_10 = lax.ppermute(compact(to_other, same), ALL, move(1, 0))
-
-    rows = panel_rows(panel_scalars, strip, coupling.reshape(RL, T, PANELS * T), lb, high, low)
+    swap = permutation(lambda xh, y, core, z, xl: (xh, y, 1 - core, z, xl))
+    flip = lambda d: permutation(lambda xh, y, core, z, xl: (xh, y, core, z ^ (d // 2), xl ^ (d % 2)))
+    cross = exchange(cross.reshape(32, T, T), PLANE).reshape(8, 4, T, T)
+    strip, cross = lax.optimization_barrier((strip, cross))
+
+    strip = exchange(strip.reshape(128, 32, T), ALL)
+    send_01, send_11 = compact((to_own[:FIRST], to_other[:FIRST]), cross)
+
+    piece = first[0]
+    for s in range(1, 8):
+        pairs = []
+        for owner in range(16):
+            t, u = owner // 4, owner % 4
+            pairs.append((t * 8 + u, (t + s // 2 * 4) * 8 + u + s % 2 * 4))
+        arrived = lax.ppermute(first[s], ALL, pairs)
+        piece = jnp.where(row // 4 * 2 + col // 4 == s, arrived, piece)
+    mine = strip.reshape(16, 8, 32, T)[:8, :PANELS]
+    held = [mine] + [lax.ppermute(mine, ALL, flip(2 * d)) for d in range(1, 4)]
+    piece, held, send_01, send_11 = lax.optimization_barrier((piece, held, send_01, send_11))
+    own_half = exchange(jnp.broadcast_to(piece[None], (64, 32, T)), CHIPS)
+    other_half = lax.ppermute(own_half, ALL, swap)
+    same, held, other_half, send_01, send_11 = lax.optimization_barrier(
+        (same, held, other_half, send_01, send_11)
+    )
+
+    held = jnp.stack(held)
+    strips = [held, lax.ppermute(held, ALL, flip(1))]
+    from_01 = lax.ppermute(send_01, ALL, move(0, 1))
+    from_11 = lax.ppermute(send_11, ALL, move(1, 1))
+    same = exchange(same.reshape(32, T, T), PLANE).reshape(8, 4, T, T)
+
+    lb, high, low = pivot(core.reshape(1), own_half, other_half, pivot_shift.reshape(PANELS, T, 1))
+    *rows, all_rows = panel_rows(panel_scalars, strips, coupling.reshape(RL, T, PANELS * T), lb, high, low)
 
     own, other = [], []
-    for j, (lo, hi) in enumerate(PIECES):
-        turn = permutation(lambda xh, y, core, z, xl: (xl ^ (j % 2), z - y + j, xh, y, core))
-        own.append(lax.ppermute(rows[lo:hi], ALL, turn))
+    for j in range(len(PIECES)):
+        turn = permutation(lambda xh, y, core, z, xl: (xl ^ core ^ xh, z - y + j, xh, y, core))
+        own.append(lax.ppermute(rows[j], ALL, turn))
         other.append(lax.ppermute(own[-1], ALL, swap))
 
-    result = front(front_scalars, rows, (same, from_01, from_10, from_11), own, other)
+    same, from_01, from_11, all_rows = lax.optimization_barrier((same, from_01, from_11, all_rows))
+    from_10 = lax.ppermute(compact((to_other[:FIRST],), same)[0], ALL, move(1, 0))
+
+    def finish(f01, f10, f11):
+        return front(front_scalars, all_rows, (same, f01, f10, f11), own, other)
+
+    def finish_rest(f01, f10, f11):
+        rest_01, rest_11 = compact((to_own[FIRST:], to_other[FIRST:]), cross)
+        rest_10 = compact((to_other[FIRST:],), same)[0]
+        rest_01 = lax.ppermute(rest_01, ALL, move(0, 1))
+        rest_11 = lax.ppermute(rest_11, ALL, move(1, 1))
+        rest_10 = lax.ppermute(rest_10, ALL, move(1, 0))
+        joined = [jnp.concatenate(pair) for pair in ((f01, rest_01), (f10, rest_10), (f11, rest_11))]
+        return finish(*joined)
+
+    ones = child_maps[:, None, :] % 16 == jnp.arange(16)[None, :, None]
+    most = jnp.max(jnp.sum(ones.astype(i32), axis=2))
+    result = lax.cond(most <= FIRST, finish, finish_rest, from_01, from_10, from_11)
     return jnp.transpose(result, (0, 2, 1, 3)).reshape(RL, 1, T, CL, 1, T)
 
 

time: 471 us -> 387 us (0.82)
  the two profiles are of different devices: /device:TPU:8 before, /device:TPU:5 now
where the time goes in v2:
time: 387 us; the launch traced here: 385 us
  starting transfers between devices  112 us (29%)
  Pallas kernels  105 us (27%)
  blocking collectives  83.5 us (22%)
  waiting for transfers between devices  72.7 us (19%)
  other arithmetic  5.32 us (1%)
  local copies, waits for them, and re-layouts  5.01 us (1%)
    all_to_all x2, blocking collectives, exchange(): return lax.all_to_all(x, axes, split_axis=0, concat_axis=0, tiled=True)  83.5 us
    ppermute x2, starting transfers between devices, per_device(): other.append(lax.ppermute(own[-1], ALL, swap))  76.7 us
    pallas_call x1, Pallas kernels, pivot(): pl.pallas_call(pivot_kernel, out_shape=(jax.ShapeDtypeStruct((PANELS, PAN...  42.3 us
    ppermute x1, waiting for transfers between devices, per_device(): from_01 = lax.ppermute(send_01, ALL, move(0, 1))  33.1 us
    pallas_call x1, Pallas kernels, front(): pl.pallas_call(front_kernel, out_shape=jax.ShapeDtypeStruct((RL, CL, T, T...  25.8 us
    all_to_all x2, waiting for transfers between devices, exchange(): return lax.all_to_all(x, axes, split_axis=0, concat_axis=0, tiled=True)  24.4 us
    pallas_call x1, Pallas kernels, panel_rows(): pl.pallas_call(panel_kernel, out_shape=[jax.ShapeDtypeStruct((hi - lo, T,...  12.7 us
    pallas_call x2, Pallas kernels, compact(): pl.pallas_call(copy_kernel, out_shape=[jax.ShapeDtypeStruct((count, 4, T,...  12.4 us
  transfers between devices with their start and end apart: 21, of which 7 were waited for; matrix products, arithmetic and copies ran while one was open for 2% of the time, Pallas kernels for 18%

profile of v2, /device:TPU:5, one launch (start us, length us, event | category | flops | bytes accessed | tf_op | source)
XLA Modules:
  0.0 384.5 jit_solution(9976160310095012432)
XLA Ops:
  0.5 1.5 fusion.25
  3.1 11.6 %pack.1 = (bf16[8,4,256,256]{3,2,1,0:T(8,128)(2,1)}, bf16[8,4,256,256]{3,2,1,0:T(8,128)(2,1)}, bf16[16,8,32,256]{3,2,1,0:T(8,128)(2,1)}, bf16[8,32,256]{2,1,0:T(8,128)(2,1)}) custom-call(s32[24]{0:T(128)} %pad_add_fusion.2.s_ref, bf16[8,2048,256]{2,1,0:T(8,128)(2,1)} %bitcast.67), custom_call_target="tpu_custom_call" | custom-call | flops 2147483648 | bytes 16777216 | tf_op jit(solution)/shard_map/pack/pallas_call | solution.py:84
  14.7 58.9 %all_to_all.20 = bf16[32,256,256]{2,1,0:T(8,128)(2,1)} all-to-all(bf16[32,256,256]{2,1,0:T(8,128)(2,1)} %bitcast.69), channel_id=1, replica_groups=mesh['xh'=2,'y1'=2,'y0'=2,'core'=2,'z1'=2,'z0'=2,'xl'=2] {'y1','y0','cor..., dimensions={0} | all-to-all | bytes 8388608 | tf_op jit(solution)/shard_map/all_to_all | solution.py:38
  73.6 6.6 %all-to-all-start.1 = ((bf16[128,32,256]{2,1,0:T(8,128)(2,1)}), bf16[128,32,256]{2,1,0:T(8,128)(2,1)S(1)}, u32[]{:S(2)}, u32[]{:S(2)}) async-start(bf16[128,32,256]{2,1,0:T(8,128)(2,1)} %bitcast.71), calls=%async_computation.1 | async-start | bytes 4194304 | tf_op jit(solution)/shard_map/all_to_all | solution.py:38
  82.5 24.3 %all-to-all-done.1 = bf16[128,32,256]{2,1,0:T(8,128)(2,1)S(1)} async-done(((bf16[128,32,256]{2,1,0:T(8,128)(2,1)}), bf16[128,32,256]{2,1,0:T(8,128)(2,1)S(1)}, u32[]{:S(2)}, u32[]{:S(2)}) %all-to-all-start.1) | async-done | bytes 2097184 | tf_op jit(solution)/shard_map/all_to_all | solution.py:38
  106.9 2.4 collective-permute-start.12
  110.4 1.3 collective-permute-start.6
  112.5 4.2 %collective-permute-done.6 = bf16[32,256]{1,0:T(8,128)(2,1)S(1)} collective-permute-done((bf16[32,256]{1,0:T(8,128)(2,1)S(1)}, bf16[32,256]{1,0:T(8,128)(2,1)S(1)}, u32[]{:S(2)}, u32[]{:S(2)}) %collective-permute-start.6) | collective-permute-done | bytes 16416 | tf_op jit(solution)/shard_map/ppermute | solution.py:421
  118.6 7.1 %compact.6 = (bf16[5,4,256,256]{3,2,1,0:T(8,128)(2,1)}, bf16[5,4,256,256]{3,2,1,0:T(8,128)(2,1)}) custom-call(s32[10]{0:T(128)} %pad_add_fusion.3.s_ref, bf16[8,4,256,256]{3,2,1,0:T(8,128)(2,1)} %bitcast.64, bf16[8,4,256,256]{3,2,1,0:T(8,128)(2,1)} %bitcast.65), custom_call_target="tpu_custom_call" | custom-call | bytes 10485760 | tf_op jit(solution)/shard_map/compact/pallas_call | solution.py:119
  125.7 6.4 %collective-permute-done.12 = bf16[8,4,32,256]{3,2,1,0:T(8,128)(2,1)S(1)} collective-permute-done((bf16[8,4,32,256]{3,2,1,0:T(8,128)(2,1)S(1)}, bf16[8,4,32,256]{3,2,1,0:T(8,128)(2,1)S(1)}, u32[]{:S(2)}, u32[]{:S(2)}) %collective-permute-start.12) | collective-permute-done | bytes 524320 | tf_op jit(solution)/shard_map/ppermute | solution.py:424
  132.2 24.7 %all_to_all.21.own_ref = bf16[64,32,256]{2,1,0:T(8,128)(2,1)S(1)} all-to-all(bf16[64,32,256]{2,1,0:T(8,128)(2,1)S(1)} %broadcast_in_dim.182), channel_id=1, replica_groups=mesh['xh'=2,'y1'=2,'y0'=2,'core'=2,'z1'=2,'z0'=2,'xl'=2] {'xh','y1','y0'..., dimensions={0} | all-to-all | bytes 2097152 | tf_op jit(solution)/shard_map/all_to_all | solution.py:38
  156.9 2.3 collective-permute-start.13
  161.6 4.8 %all-to-all-start.3 = ((bf16[32,256,256]{2,1,0:T(8,128)(2,1)}), bf16[32,256,256]{2,1,0:T(8,128)(2,1)}, u32[]{:S(2)}, u32[]{:S(2)}) async-start(bf16[32,256,256]{2,1,0:T(8,128)(2,1)} %bitcast.68), calls=%async_computation.3 | async-start | bytes 8388608 | tf_op jit(solution)/shard_map/all_to_all | solution.py:38
  169.3 42.3 %pivot_factor.1 = (bf16[4,1024,256]{2,1,0:T(8,128)(2,1)}, bf16[4,256,256]{2,1,0:T(8,128)(2,1)}, bf16[4,256,256]{2,1,0:T(8,128)(2,1)}) custom-call(s32[1]{0:T(128)} %bitcast.25.core_ref, bf16[64,32,256]{2,1,0:T(8,128)(2,1)} %copy-done.2, bf16[64,32,256]{2,1,0:T(8,128)(2,1)} %collective-permute-done.13.other_ref, f32[4,256,1]{2,1,0:T(8,128)} %reshape.157.shift_ref), custom_call_target="tpu_custom_call" | custom-call | flops 44999999488 | bytes 4194304 | tf_op jit(solution)/shard_map/pivot_factor/pallas_call | solution.py:218
  211.6 2.1 collective-permute-done.16.refs_1_
  213.7 12.7 %panel_rows.1 = (bf16[4,256,1024]{2,1,0:T(8,128)(2,1)}, bf16[3,256,1024]{2,1,0:T(8,128)(2,1)}, bf16[7,256,1024]{2,1,0:T(8,128)(2,1)}) custom-call(s32[16]{0:T(128)} %pad_add_fusion.4.s_ref, bf16[4,8,4,32,256]{4,3,2,1,0:T(8,128)(2,1)} %copy-done.1, bf16[4,8,4,32,256]{4,3,2,1,0:T(8,128)(2,1)} %collective-permute-done.16.refs_1_, ...), custom_call_target="tpu_custom_call" | custom-call | flops 8000000000 | bytes 12582912 | tf_op jit(solution)/shard_map/panel_rows/pallas_call | solution.py:271
  226.4 2.4 collective-permute-start.18
  228.8 7.7 %collective-permute-start.19 = (bf16[3,256,1024]{2,1,0:T(8,128)(2,1)}, bf16[3,256,1024]{2,1,0:T(8,128)(2,1)}, u32[]{:S(2)}, u32[]{:S(2)}) collective-permute-start(bf16[3,256,1024]{2,1,0:T(8,128)(2,1)} %get-tuple-element.144), channel_id=1, source_target_pairs={{0,16},{1,80},{2,32},{3,96},{4,48},{5,112},{6,0},{7,64},{8,81},{9,... | collective-permute-start | bytes 4718600 | tf_op jit(solution)/shard_map/ppermute | solution.py:444
  236.7 33.1 %collective-permute-done.14 = bf16[5,4,256,256]{3,2,1,0:T(8,128)(2,1)S(1)} collective-permute-done((bf16[5,4,256,256]{3,2,1,0:T(8,128)(2,1)}, bf16[5,4,256,256]{3,2,1,0:T(8,128)(2,1)S(1)}, u32[]{:S(2)}, u32[]{:S(2)}) %collective-permute-start.14) | collective-permute-done | bytes 2621472 | tf_op jit(solution)/shard_map/ppermute | solution.py:434
  269.8 5.2 %compact.7 = bf16[5,4,256,256]{3,2,1,0:T(8,128)(2,1)} custom-call(s32[5]{0:T(128)S(1)} %bitcast.77, bf16[8,4,256,256]{3,2,1,0:T(8,128)(2,1)} %bitcast.16.refs_0_), custom_call_target="tpu_custom_call" | custom-call | bytes 5242880 | tf_op jit(solution)/shard_map/compact/pallas_call | solution.py:119
  279.7 75.6 %collective-permute-start.21 = (bf16[3,256,1024]{2,1,0:T(8,128)(2,1)}, bf16[3,256,1024]{2,1,0:T(8,128)(2,1)}, u32[]{:S(2)}, u32[]{:S(2)}) collective-permute-start(bf16[3,256,1024]{2,1,0:T(8,128)(2,1)} %collective-permute-done.19), channel_id=1, source_target_pairs={{0,8},{1,9},{2,10},{3,11},{4,12},{5,13},{6,14},{7,15},{8,0},{9,1},... | collective-permute-start | bytes 4718600 | tf_op jit(solution)/shard_map/ppermute | solution.py:445
  356.3 2.3 collective-permute-done.21
  358.7 25.8 %conditional.1 = (bf16[7,14,256,256]{3,2,1,0:T(8,128)(2,1)}) conditional(s32[]{:T(128)} %convert_element_type.30, (s32[7]{0:T(128)S(1)}, s32[7]{0:T(128)S(1)}, bf16[8,4,256,256]{3,2,1,0:T(8,128)(2,1)}, bf16[5,4,256,256]{3,2,1,0:T(8,128)(2,1)S(1)}, bf16[8,4,256,256]{3,2,1,0:T(8,128)(2,1)}, /*index=5*/bf16[5,4,256,256]{3,2,1,0:T(8,128)(2,1)}, ...), branch_computations={%region_19.20_spmd, %region_20.21_spmd} | conditional | flops 13158842368 | bytes 114295096 | solution.py:464
  358.7 25.8 %front.3 = bf16[7,14,256,256]{3,2,1,0:T(8,128)(2,1)} custom-call(s32[122]{0:T(128)S(1)} %get-tuple-element.69.s_ref, bf16[7,256,1024]{2,1,0:T(8,128)(2,1)} %get-tuple-element.70.rows_ref, bf16[8,4,256,256]{3,2,1,0:T(8,128)(2,1)} %get-tuple-element.71.refs_0_, bf16[5,4,256,256]{3,2,1,0:T(8,128)(2,1)S(1)} %get-tuple-element.72.refs_1_, ...), custom_call_target="tpu_custom_call" | custom-call | flops 13153337344 | bytes 41943040 | tf_op jit(solution)/shard_map/cond/branch_1_fun/front/pallas_call | solution.py:326
  (96 shorter events, 18.4 us)
Async XLA Ops:
  73.6 33.3 %all-to-all-start.1 = ((bf16[128,32,256]{2,1,0:T(8,128)(2,1)}), bf16[128,32,256]{2,1,0:T(8,128)(2,1)S(1)}, u32[]{:S(2)}, u32[]{:S(2)}) async-start(bf16[128,32,256]{2,1,0:T(8,128)(2,1)} %bitcast.71), calls=%async_computation.1 | async-start | bytes 4194304 | tf_op jit(solution)/shard_map/all_to_all | solution.py:38
  80.3 29.1 %collective-permute-start.9 = (bf16[32,256]{1,0:T(8,128)(2,1)S(1)}, bf16[32,256]{1,0:T(8,128)(2,1)S(1)}, u32[]{:S(2)}, u32[]{:S(2)}) collective-permute-start(bf16[32,256]{1,0:T(8,128)(2,1)S(1)} %get-tuple-element.161), channel_id=1, source_target_pairs={{0,4},{1,5},{2,6},{3,7},{8,12},{9,13},{10,14},{11,15},{16,20},{17,... | collective-permute-start | bytes 49160 | tf_op jit(solution)/shard_map/ppermute | solution.py:421
  80.9 29.4 %collective-permute-start.8 = (bf16[32,256]{1,0:T(8,128)(2,1)S(1)}, bf16[32,256]{1,0:T(8,128)(2,1)S(1)}, u32[]{:S(2)}, u32[]{:S(2)}) collective-permute-start(bf16[32,256]{1,0:T(8,128)(2,1)S(1)} %get-tuple-element.162), channel_id=1, source_target_pairs={{0,32},{1,33},{2,34},{3,35},{8,40},{9,41},{10,42},{11,43},{16,48},... | collective-permute-start | bytes 49160 | tf_op jit(solution)/shard_map/ppermute | solution.py:421
  81.6 30.1 %collective-permute-start.7 = (bf16[32,256]{1,0:T(8,128)(2,1)S(1)}, bf16[32,256]{1,0:T(8,128)(2,1)S(1)}, u32[]{:S(2)}, u32[]{:S(2)}) collective-permute-start(bf16[32,256]{1,0:T(8,128)(2,1)S(1)} %get-tuple-element.163), channel_id=1, source_target_pairs={{0,36},{1,37},{2,38},{3,39},{8,44},{9,45},{10,46},{11,47},{16,52},... | collective-permute-start | bytes 49160 | tf_op jit(solution)/shard_map/ppermute | solution.py:421
  106.9 25.2 %collective-permute-start.12 = (bf16[8,4,32,256]{3,2,1,0:T(8,128)(2,1)S(1)}, bf16[8,4,32,256]{3,2,1,0:T(8,128)(2,1)S(1)}, u32[]{:S(2)}, u32[]{:S(2)}) collective-permute-start(bf16[8,4,32,256]{3,2,1,0:T(8,128)(2,1)S(1)} %slice.105), channel_id=1, source_target_pairs={{0,6},{1,7},{2,4},{3,5},{4,2},{5,3},{6,0},{7,1},{8,14},{9,15},{10,... | collective-permute-start | bytes 1572872 | tf_op jit(solution)/shard_map/ppermute | solution.py:424
  109.3 22.8 %collective-permute-start.11 = (bf16[8,4,32,256]{3,2,1,0:T(8,128)(2,1)S(1)}, bf16[8,4,32,256]{3,2,1,0:T(8,128)(2,1)S(1)}, u32[]{:S(2)}, u32[]{:S(2)}) collective-permute-start(bf16[8,4,32,256]{3,2,1,0:T(8,128)(2,1)S(1)} %slice.105), channel_id=1, source_target_pairs={{0,4},{1,5},{2,6},{3,7},{4,0},{5,1},{6,2},{7,3},{8,12},{9,13},{10,... | collective-permute-start | bytes 1572872 | tf_op jit(solution)/shard_map/ppermute | solution.py:424
  109.3 22.8 %collective-permute-start.10 = (bf16[8,4,32,256]{3,2,1,0:T(8,128)(2,1)S(1)}, bf16[8,4,32,256]{3,2,1,0:T(8,128)(2,1)S(1)}, u32[]{:S(2)}, u32[]{:S(2)}) collective-permute-start(bf16[8,4,32,256]{3,2,1,0:T(8,128)(2,1)S(1)} %slice.105), channel_id=1, source_target_pairs={{0,2},{1,3},{2,0},{3,1},{4,6},{5,7},{6,4},{7,5},{8,10},{9,11},{10,... | collective-permute-start | bytes 1572872 | tf_op jit(solution)/shard_map/ppermute | solution.py:424
  110.4 6.3 %collective-permute-start.6 = (bf16[32,256]{1,0:T(8,128)(2,1)S(1)}, bf16[32,256]{1,0:T(8,128)(2,1)S(1)}, u32[]{:S(2)}, u32[]{:S(2)}) collective-permute-start(bf16[32,256]{1,0:T(8,128)(2,1)S(1)} %get-tuple-element.164), channel_id=1, source_target_pairs={{0,64},{1,65},{2,66},{3,67},{8,72},{9,73},{10,74},{11,75},{16,80},... | collective-permute-start | bytes 49160 | tf_op jit(solution)/shard_map/ppermute | solution.py:421
  111.7 5.6 %collective-permute-start.5 = (bf16[32,256]{1,0:T(8,128)(2,1)S(1)}, bf16[32,256]{1,0:T(8,128)(2,1)S(1)}, u32[]{:S(2)}, u32[]{:S(2)}) collective-permute-start(bf16[32,256]{1,0:T(8,128)(2,1)S(1)} %get-tuple-element.165), channel_id=1, source_target_pairs={{0,68},{1,69},{2,70},{3,71},{8,76},{9,77},{10,78},{11,79},{16,84},... | collective-permute-start | bytes 49160 | tf_op jit(solution)/shard_map/ppermute | solution.py:421
  116.7 1.9 collective-permute-start.4
  117.3 1.2 collective-permute-start.3
  125.7 33.6 %copy-start.5 = (f32[1024]{0:T(1024)S(1)}, f32[1024]{0:T(1024)}, u32[]{:S(2)}) copy-start(f32[1024]{0:T(1024)} %param.9) | copy-start | bytes 12292
  156.9 4.7 %collective-permute-start.13 = (bf16[64,32,256]{2,1,0:T(8,128)(2,1)S(1)}, bf16[64,32,256]{2,1,0:T(8,128)(2,1)}, u32[]{:S(2)}, u32[]{:S(2)}) collective-permute-start(bf16[64,32,256]{2,1,0:T(8,128)(2,1)S(1)} %all_to_all.21.own_ref), channel_id=1, source_target_pairs={{0,8},{1,9},{2,10},{3,11},{4,12},{5,13},{6,14},{7,15},{8,0},{9,1},... | collective-permute-start | bytes 3145736 | tf_op jit(solution)/shard_map/ppermute | solution.py:427
  161.6 108.2 %all-to-all-start.3 = ((bf16[32,256,256]{2,1,0:T(8,128)(2,1)}), bf16[32,256,256]{2,1,0:T(8,128)(2,1)}, u32[]{:S(2)}, u32[]{:S(2)}) async-start(bf16[32,256,256]{2,1,0:T(8,128)(2,1)} %bitcast.68), calls=%async_computation.3 | async-start | bytes 8388608 | tf_op jit(solution)/shard_map/all_to_all | solution.py:38
  166.7 44.9 %copy-start.1 = (bf16[4,8,4,32,256]{4,3,2,1,0:T(8,128)(2,1)}, bf16[4,8,4,32,256]{4,3,2,1,0:T(8,128)(2,1)S(1)}, u32[]{:S(2)}) copy-start(bf16[4,8,4,32,256]{4,3,2,1,0:T(8,128)(2,1)S(1)} %pad_maximum_fusion.3.refs_0_) | copy-start | bytes 6291460
  166.7 47.0 %collective-permute-start.16 = (bf16[4,8,4,32,256]{4,3,2,1,0:T(8,128)(2,1)S(1)}, bf16[4,8,4,32,256]{4,3,2,1,0:T(8,128)(2,1)}, u32[]{:S(2)}, u32[]{:S(2)}) collective-permute-start(bf16[4,8,4,32,256]{4,3,2,1,0:T(8,128)(2,1)S(1)} %pad_maximum_fusion.3.refs_0_), channel_id=1, source_target_pairs={{0,1},{1,0},{2,3},{3,2},{4,5},{5,4},{6,7},{7,6},{8,9},{9,8},{10,11... | collective-permute-start | bytes 6291464 | tf_op jit(solution)/shard_map/ppermute | solution.py:433
  167.4 102.3 %collective-permute-start.14 = (bf16[5,4,256,256]{3,2,1,0:T(8,128)(2,1)}, bf16[5,4,256,256]{3,2,1,0:T(8,128)(2,1)S(1)}, u32[]{:S(2)}, u32[]{:S(2)}) collective-permute-start(bf16[5,4,256,256]{3,2,1,0:T(8,128)(2,1)} %get-tuple-element.128), channel_id=1, source_target_pairs={{0,1},{1,0},{2,3},{3,2},{4,5},{5,4},{6,7},{7,6},{8,9},{9,8},{10,11... | collective-permute-start | bytes 7864328 | tf_op jit(solution)/shard_map/ppermute | solution.py:434
  168.9 100.9 %collective-permute-start.15 = (bf16[5,4,256,256]{3,2,1,0:T(8,128)(2,1)S(1)}, bf16[5,4,256,256]{3,2,1,0:T(8,128)(2,1)}, u32[]{:S(2)}, u32[]{:S(2)}) collective-permute-start(bf16[5,4,256,256]{3,2,1,0:T(8,128)(2,1)S(1)} %copy-done.7), channel_id=1, source_target_pairs={{0,65},{1,64},{2,67},{3,66},{4,69},{5,68},{6,71},{7,70},{8,73},{9,... | collective-permute-start | bytes 7864328 | tf_op jit(solution)/shard_map/ppermute | solution.py:435
  213.7 22.9 %copy-start.4 = (s32[2,64]{1,0:T(2,128)S(1)}, s32[2,64]{1,0:T(2,128)}, u32[]{:S(2)}) copy-start(s32[2,64]{1,0:T(2,128)} %param.7) | copy-start | bytes 1540
  226.4 51.9 %collective-permute-start.18 = (bf16[4,256,1024]{2,1,0:T(8,128)(2,1)}, bf16[4,256,1024]{2,1,0:T(8,128)(2,1)}, u32[]{:S(2)}, u32[]{:S(2)}) collective-permute-start(bf16[4,256,1024]{2,1,0:T(8,128)(2,1)} %get-tuple-element.143), channel_id=1, source_target_pairs={{0,0},{1,64},{2,16},{3,80},{4,32},{5,96},{6,48},{7,112},{8,65},{9,... | collective-permute-start | bytes 6291464 | tf_op jit(solution)/shard_map/ppermute | solution.py:444
  228.8 51.0 %collective-permute-start.19 = (bf16[3,256,1024]{2,1,0:T(8,128)(2,1)}, bf16[3,256,1024]{2,1,0:T(8,128)(2,1)}, u32[]{:S(2)}, u32[]{:S(2)}) collective-permute-start(bf16[3,256,1024]{2,1,0:T(8,128)(2,1)} %get-tuple-element.144), channel_id=1, source_target_pairs={{0,16},{1,80},{2,32},{3,96},{4,48},{5,112},{6,0},{7,64},{8,81},{9,... | collective-permute-start | bytes 4718600 | tf_op jit(solution)/shard_map/ppermute | solution.py:444
  275.0 83.6 %collective-permute-start.17 = (bf16[5,4,256,256]{3,2,1,0:T(8,128)(2,1)}, bf16[5,4,256,256]{3,2,1,0:T(8,128)(2,1)}, u32[]{:S(2)}, u32[]{:S(2)}) collective-permute-start(bf16[5,4,256,256]{3,2,1,0:T(8,128)(2,1)} %compact.7), channel_id=1, source_target_pairs={{0,64},{1,65},{2,66},{3,67},{4,68},{5,69},{6,70},{7,71},{8,72},{9,... | collective-permute-start | bytes 7864328 | tf_op jit(solution)/shard_map/ppermute | solution.py:448
  278.3 80.4 %collective-permute-start.20 = (bf16[4,256,1024]{2,1,0:T(8,128)(2,1)}, bf16[4,256,1024]{2,1,0:T(8,128)(2,1)}, u32[]{:S(2)}, u32[]{:S(2)}) collective-permute-start(bf16[4,256,1024]{2,1,0:T(8,128)(2,1)} %collective-permute-done.18), channel_id=1, source_target_pairs={{0,8},{1,9},{2,10},{3,11},{4,12},{5,13},{6,14},{7,15},{8,0},{9,1},... | collective-permute-start | bytes 6291464 | tf_op jit(solution)/shard_map/ppermute | solution.py:445
  279.7 78.9 %collective-permute-start.21 = (bf16[3,256,1024]{2,1,0:T(8,128)(2,1)}, bf16[3,256,1024]{2,1,0:T(8,128)(2,1)}, u32[]{:S(2)}, u32[]{:S(2)}) collective-permute-start(bf16[3,256,1024]{2,1,0:T(8,128)(2,1)} %collective-permute-done.19), channel_id=1, source_target_pairs={{0,8},{1,9},{2,10},{3,11},{4,12},{5,13},{6,14},{7,15},{8,0},{9,1},... | collective-permute-start | bytes 4718600 | tf_op jit(solution)/shard_map/ppermute | solution.py:445
  (3 other events, 13.8 us)

commit v3 on v2

--- a/solution.py
+++ b/solution.py
@@ -59,47 +59,42 @@
     return dot_t(high, inv_high) + (dot_t(high, inv_low) + dot_t(low, inv_high))
 
 
-def pack_kernel(s_ref, x_ref, same_ref, cross_ref, strip_ref, first_ref, moved):
-    rows = lax.broadcasted_iota(i32, (T, T), 0)
-    cols = lax.broadcasted_iota(i32, (T, T), 1)
-    pick = jnp.where((rows % 32) * 8 + rows // 32 == cols, 1.0, 0.0).astype(bf16)
+def pack_kernel(s_ref, x_ref, out_ref, *strip_refs):
+    count = 5 if strip_refs else 4
+    rows = lax.broadcasted_iota(i32, (32 * count, T), 0)
+    cols = lax.broadcasted_iota(i32, (32 * count, T), 1)
+    tile = sum(jnp.where(rows // 32 == z, s_ref[16 + z], 0) for z in range(4))
+    pick = jnp.where((rows % 32) * 8 + tile == cols, 1.0, 0.0).astype(bf16)
     for g in range(8):
         part = x_ref[0, g * T : (g + 1) * T, :]
         tiles = jnp.dot(pick, part, preferred_element_type=f32).astype(bf16)
-        moved[g % 2] = tiles
-        strip_ref[0, g] = tiles[:32]
-        for e, out_ref in enumerate((same_ref, cross_ref)):
-            for z in range(4):
-                at = pl.ds(pl.multiple_of(s_ref[16 + 4 * e + z] * 32, 32), 32)
-                out_ref[0, z, g * 32 : (g + 1) * 32, :] = moved[g % 2, at, :]
-
-    @pl.when(pl.program_id(0) == 0)
-    def _():
-        first_ref[...] = strip_ref[0]
-
-
-def pack(scalars, tiles):
-    shape = jax.ShapeDtypeStruct((8, 4, T, T), bf16)
-    spec = pl.BlockSpec((1, 4, T, T), lambda a, s: (s[a], 0, 0, 0))
+        for z in range(4):
+            out_ref[0, z, g * 32 : (g + 1) * 32, :] = tiles[z * 32 : (z + 1) * 32]
+        if strip_refs:
+            strip_refs[0][0, g] = tiles[128:]
+    if strip_refs:
+
+        @pl.when(pl.program_id(0) == 0)
+        def _():
+            strip_refs[1][...] = strip_refs[0][0]
+
+
+def pack(scalars, tiles, with_strip):
+    shapes = [(8, 4, T, T), (16, 8, 32, T), (8, 32, T)]
+    specs = [
+        pl.BlockSpec((1, 4, T, T), lambda a, s: (s[a], 0, 0, 0)),
+        pl.BlockSpec((1, 8, 32, T), lambda a, s: (s[8 + a], 0, 0, 0)),
+        pl.BlockSpec((8, 32, T), lambda a, s: (0, 0, 0)),
+    ]
+    count = 3 if with_strip else 1
     return pl.pallas_call(
         pack_kernel,
-        out_shape=(
-            shape,
-            shape,
-            jax.ShapeDtypeStruct((16, 8, 32, T), bf16),
-            jax.ShapeDtypeStruct((8, 32, T), bf16),
-        ),
+        out_shape=[jax.ShapeDtypeStruct(shape, bf16) for shape in shapes[:count]],
         grid_spec=pltpu.PrefetchScalarGridSpec(
             num_scalar_prefetch=1,
             grid=(8,),
             in_specs=[pl.BlockSpec((1, 8 * T, T), lambda a, s: (a, 0, 0))],
-            out_specs=[
-                spec,
-                spec,
-                pl.BlockSpec((1, 8, 32, T), lambda a, s: (s[8 + a], 0, 0, 0)),
-                pl.BlockSpec((8, 32, T), lambda a, s: (0, 0, 0)),
-            ],
-            scratch_shapes=[pltpu.VMEM((2, T, T), bf16)],
+            out_specs=specs[:count],
         ),
         compiler_params=pltpu.CompilerParams(vmem_limit_bytes=VMEM),
         cost_estimate=pl.CostEstimate(flops=2 * 64 * T**3, bytes_accessed=1 << 24, transcendentals=0),
@@ -359,9 +354,7 @@
     col_to = jnp.sum(jnp.where(eight[None, :] == col, own_map, 0), axis=1)
     by_to = lambda slots: jnp.sum(jnp.where(col_to[None, :] % 8 == slots[:, None], eight[None, :], 0), axis=1)
     same_to = 2 * jnp.arange(4) + xl
-    pack_scalars = jnp.concatenate(
-        [row_to % 8, row_to % 16, by_to(same_to), by_to(same_to ^ 1)]
-    ).astype(i32)
+    pack_scalars = lambda to: jnp.concatenate([row_to % 8, row_to % 16, by_to(to)]).astype(i32)
 
     both = jnp.stack([child_maps[xh], child_maps[1 - xh]])
     at = jnp.arange(64)
@@ -401,7 +394,8 @@
     ).astype(i32)
 
     tiles = children.reshape(8, 8 * T, T)
-    same, cross, strip, first = pack(pack_scalars, tiles)
+    (cross,) = pack(pack_scalars(same_to ^ 1), tiles, False)
+    same, strip, first = pack(pack_scalars(same_to), tiles, True)
 
     move = lambda f, e: permutation(lambda xh, y, core, z, xl: (xh ^ f, y, core, z, xl ^ e))
     swap = permutation(lambda xh, y, core, z, xl: (xh, y, 1 - core, z, xl))
@@ -440,7 +434,9 @@
 
     own, other = [], []
     for j in range(len(PIECES)):
-        turn = permutation(lambda xh, y, core, z, xl: (xl ^ core ^ xh, z - y + j, xh, y, core))
+        turn = permutation(
+            lambda xh, y, core, z, xl: (xl ^ core ^ xh, z - y + 2 * j + core + 2 * xh, xh, y, core)
+        )
         own.append(lax.ppermute(rows[j], ALL, turn))
         other.append(lax.ppermute(own[-1], ALL, swap))
 

time: 387 us -> 366 us (0.946)
  the two profiles are of different devices: /device:TPU:5 before, /device:TPU:8 now
where the time goes in v3:
time: 366 us; the launch traced here: 364 us
  waiting for transfers between devices  162 us (44%)
  Pallas kernels  111 us (30%)
  starting transfers between devices  57.4 us (16%)
  blocking collectives  22.6 us (6%)
  other arithmetic  5.45 us (1%)
  local copies, waits for them, and re-layouts  4.46 us (1%)
    all_to_all x3, waiting for transfers between devices, exchange(): return lax.all_to_all(x, axes, split_axis=0, concat_axis=0, tiled=True)  61.7 us
    ppermute x1, waiting for transfers between devices, per_device(): lax.ppermute(compact((to_other[:FIRST],), same)[0], ALL, move(1, 0))  49.1 us
    pallas_call x1, Pallas kernels, pivot(): pl.pallas_call(pivot_kernel, out_shape=(jax.ShapeDtypeStruct((PANELS, PAN...  42.2 us
    ppermute x1, waiting for transfers between devices, per_device(): from_01 = lax.ppermute(send_01, ALL, move(0, 1))  35.6 us
    pallas_call x1, Pallas kernels, front(): pl.pallas_call(front_kernel, out_shape=jax.ShapeDtypeStruct((RL, CL, T, T...  26.1 us
    all_to_all x3, starting transfers between devices, exchange(): return lax.all_to_all(x, axes, split_axis=0, concat_axis=0, tiled=True)  24 us
    all_to_all x1, blocking collectives, exchange(): return lax.all_to_all(x, axes, split_axis=0, concat_axis=0, tiled=True)  22.6 us
    pallas_call x2, Pallas kernels, pack(): pl.pallas_call(pack_kernel, out_shape=[jax.ShapeDtypeStruct(shape, bf16)...  19 us
  transfers between devices with their start and end apart: 22, of which 10 were waited for; matrix products, arithmetic and copies ran while one was open for 2% of the time, Pallas kernels for 21%

profile of v3, /device:TPU:8, one launch (start us, length us, event | category | flops | bytes accessed | tf_op | source)
XLA Modules:
  0.0 364.1 jit_solution(8126367163626113816)
XLA Ops:
  3.1 9.2 %pack.3 = bf16[8,4,256,256]{3,2,1,0:T(8,128)(2,1)} custom-call(s32[20]{0:T(128)} %get-tuple-element.173.s_ref, bf16[8,2048,256]{2,1,0:T(8,128)(2,1)} %bitcast.64), custom_call_target="tpu_custom_call" | custom-call | flops 2147483648 | bytes 16777216 | tf_op jit(solution)/shard_map/pack/pallas_call | solution.py:90
  12.3 8.6 %all-to-all-start = ((bf16[32,256,256]{2,1,0:T(8,128)(2,1)}), bf16[32,256,256]{2,1,0:T(8,128)(2,1)}, u32[]{:S(2)}, u32[]{:S(2)}) async-start(bf16[32,256,256]{2,1,0:T(8,128)(2,1)} %bitcast.66), calls=%async_computation | async-start | bytes 8388608 | tf_op jit(solution)/shard_map/all_to_all | solution.py:38
  20.9 9.8 %pack.2 = (bf16[8,4,256,256]{3,2,1,0:T(8,128)(2,1)}, bf16[16,8,32,256]{3,2,1,0:T(8,128)(2,1)}, bf16[8,32,256]{2,1,0:T(8,128)(2,1)}) custom-call(s32[20]{0:T(128)} %get-tuple-element.174.s_ref, bf16[8,2048,256]{2,1,0:T(8,128)(2,1)} %bitcast.65), custom_call_target="tpu_custom_call" | custom-call | flops 2147483648 | bytes 16777216 | tf_op jit(solution)/shard_map/pack/pallas_call | solution.py:90
  30.8 40.7 %all-to-all-done = bf16[32,256,256]{2,1,0:T(8,128)(2,1)} async-done(((bf16[32,256,256]{2,1,0:T(8,128)(2,1)}), bf16[32,256,256]{2,1,0:T(8,128)(2,1)}, u32[]{:S(2)}, u32[]{:S(2)}) %all-to-all-start) | async-done | bytes 4194336 | tf_op jit(solution)/shard_map/all_to_all | solution.py:38
  71.5 9.7 %all-to-all-start.1 = ((bf16[128,32,256]{2,1,0:T(8,128)(2,1)}), bf16[128,32,256]{2,1,0:T(8,128)(2,1)S(1)}, u32[]{:S(2)}, u32[]{:S(2)}) async-start(bf16[128,32,256]{2,1,0:T(8,128)(2,1)} %bitcast.69), calls=%async_computation.1 | async-start | bytes 4194304 | tf_op jit(solution)/shard_map/all_to_all | solution.py:38
  81.2 5.3 %collective-permute-start.9 = (bf16[32,256]{1,0:T(8,128)(2,1)S(1)}, bf16[32,256]{1,0:T(8,128)(2,1)S(1)}, u32[]{:S(2)}, u32[]{:S(2)}) collective-permute-start(bf16[32,256]{1,0:T(8,128)(2,1)S(1)} %get-tuple-element.159), channel_id=1, source_target_pairs={{0,4},{1,5},{2,6},{3,7},{8,12},{9,13},{10,14},{11,15},{16,20},{17,... | collective-permute-start | bytes 49160 | tf_op jit(solution)/shard_map/ppermute | solution.py:415
  89.8 21.0 %all-to-all-done.1 = bf16[128,32,256]{2,1,0:T(8,128)(2,1)S(1)} async-done(((bf16[128,32,256]{2,1,0:T(8,128)(2,1)}), bf16[128,32,256]{2,1,0:T(8,128)(2,1)S(1)}, u32[]{:S(2)}, u32[]{:S(2)}) %all-to-all-start.1) | async-done | bytes 2097184 | tf_op jit(solution)/shard_map/all_to_all | solution.py:38
  112.6 2.3 collective-permute-start.10
  115.1 2.9 collective-permute-start.6
  124.0 6.6 %compact.6 = (bf16[5,4,256,256]{3,2,1,0:T(8,128)(2,1)}, bf16[5,4,256,256]{3,2,1,0:T(8,128)(2,1)}) custom-call(s32[10]{0:T(128)} %pad_add_fusion.5.s_ref, bf16[8,4,256,256]{3,2,1,0:T(8,128)(2,1)} %bitcast.4.refs_0_.refs_1_, bf16[8,4,256,256]{3,2,1,0:T(8,128)(2,1)} %bitcast.4.refs_0_.refs_1_), custom_call_target="tpu_custom_call" | custom-call | bytes 10485760 | tf_op jit(solution)/shard_map/compact/pallas_call | solution.py:114
  130.6 6.0 %collective-permute-done.12 = bf16[8,4,32,256]{3,2,1,0:T(8,128)(2,1)S(1)} collective-permute-done((bf16[8,4,32,256]{3,2,1,0:T(8,128)(2,1)S(1)}, bf16[8,4,32,256]{3,2,1,0:T(8,128)(2,1)S(1)}, u32[]{:S(2)}, u32[]{:S(2)}) %collective-permute-start.12) | collective-permute-done | bytes 524320 | tf_op jit(solution)/shard_map/ppermute | solution.py:418
  137.4 22.6 %all_to_all.20.own_ref = bf16[64,32,256]{2,1,0:T(8,128)(2,1)S(1)} all-to-all(bf16[64,32,256]{2,1,0:T(8,128)(2,1)S(1)} %broadcast_in_dim.182), channel_id=1, replica_groups=mesh['xh'=2,'y1'=2,'y0'=2,'core'=2,'z1'=2,'z0'=2,'xl'=2] {'xh','y1','y0'..., dimensions={0} | all-to-all | bytes 2097152 | tf_op jit(solution)/shard_map/all_to_all | solution.py:38
  162.8 5.7 %all-to-all-start.3 = ((bf16[32,256,256]{2,1,0:T(8,128)(2,1)}), bf16[32,256,256]{2,1,0:T(8,128)(2,1)}, u32[]{:S(2)}, u32[]{:S(2)}) async-start(bf16[32,256,256]{2,1,0:T(8,128)(2,1)} %bitcast.67), calls=%async_computation.3 | async-start | bytes 8388608 | tf_op jit(solution)/shard_map/all_to_all | solution.py:38
  172.5 42.2 %pivot_factor.1 = (bf16[4,1024,256]{2,1,0:T(8,128)(2,1)}, bf16[4,256,256]{2,1,0:T(8,128)(2,1)}, bf16[4,256,256]{2,1,0:T(8,128)(2,1)}) custom-call(s32[1]{0:T(128)} %bitcast.25.core_ref, bf16[64,32,256]{2,1,0:T(8,128)(2,1)} %copy-done.1, bf16[64,32,256]{2,1,0:T(8,128)(2,1)} %collective-permute-done.13.other_ref, f32[4,256,1]{2,1,0:T(8,128)} %reshape.157.shift_ref), custom_call_target="tpu_custom_call" | custom-call | flops 44999999488 | bytes 4194304 | tf_op jit(solution)/shard_map/pivot_factor/pallas_call | solution.py:213
  214.7 2.8 collective-permute-done.16.refs_1_
  217.5 12.7 %panel_rows.1 = (bf16[4,256,1024]{2,1,0:T(8,128)(2,1)}, bf16[3,256,1024]{2,1,0:T(8,128)(2,1)}, bf16[7,256,1024]{2,1,0:T(8,128)(2,1)}) custom-call(s32[16]{0:T(128)} %pad_add_fusion.6.s_ref, bf16[4,8,4,32,256]{4,3,2,1,0:T(8,128)(2,1)} %copy-done, bf16[4,8,4,32,256]{4,3,2,1,0:T(8,128)(2,1)} %collective-permute-done.16.refs_1_, bf16[7,256,1024]{2,1,0:T(8,128)(2,1)} %bitcast.77, ...), custom_call_target="tpu_custom_call" | custom-call | flops 8000000000 | bytes 12582912 | tf_op jit(solution)/shard_map/panel_rows/pallas_call | solution.py:266
  230.1 4.9 %collective-permute-start.18 = (bf16[4,256,1024]{2,1,0:T(8,128)(2,1)}, bf16[4,256,1024]{2,1,0:T(8,128)(2,1)}, u32[]{:S(2)}, u32[]{:S(2)}) collective-permute-start(bf16[4,256,1024]{2,1,0:T(8,128)(2,1)} %get-tuple-element.141), channel_id=1, source_target_pairs={{0,0},{1,64},{2,16},{3,80},{4,32},{5,96},{6,48},{7,112},{8,81},{9,... | collective-permute-start | bytes 6291464 | tf_op jit(solution)/shard_map/ppermute | solution.py:440
  237.2 35.6 %collective-permute-done.14 = bf16[5,4,256,256]{3,2,1,0:T(8,128)(2,1)S(1)} collective-permute-done((bf16[5,4,256,256]{3,2,1,0:T(8,128)(2,1)}, bf16[5,4,256,256]{3,2,1,0:T(8,128)(2,1)S(1)}, u32[]{:S(2)}, u32[]{:S(2)}) %collective-permute-start.14) | collective-permute-done | bytes 2621472 | tf_op jit(solution)/shard_map/ppermute | solution.py:428
  272.7 4.8 %compact.7 = bf16[5,4,256,256]{3,2,1,0:T(8,128)(2,1)} custom-call(s32[5]{0:T(128)S(1)} %bitcast.75, bf16[8,4,256,256]{3,2,1,0:T(8,128)(2,1)} %bitcast.16.refs_0_), custom_call_target="tpu_custom_call" | custom-call | bytes 5242880 | tf_op jit(solution)/shard_map/compact/pallas_call | solution.py:114
  277.5 2.5 collective-permute-start.17
  284.1 4.7 %collective-permute-done.21 = bf16[3,256,1024]{2,1,0:T(8,128)(2,1)} collective-permute-done((bf16[3,256,1024]{2,1,0:T(8,128)(2,1)}, bf16[3,256,1024]{2,1,0:T(8,128)(2,1)}, u32[]{:S(2)}, u32[]{:S(2)}) %collective-permute-start.21) | collective-permute-done | bytes 1572896 | tf_op jit(solution)/shard_map/ppermute | solution.py:441
  288.9 49.1 %collective-permute-done.17 = bf16[5,4,256,256]{3,2,1,0:T(8,128)(2,1)} collective-permute-done((bf16[5,4,256,256]{3,2,1,0:T(8,128)(2,1)}, bf16[5,4,256,256]{3,2,1,0:T(8,128)(2,1)}, u32[]{:S(2)}, u32[]{:S(2)}) %collective-permute-start.17) | collective-permute-done | bytes 2621472 | tf_op jit(solution)/shard_map/ppermute | solution.py:444
  338.0 26.1 %conditional.1 = (bf16[7,14,256,256]{3,2,1,0:T(8,128)(2,1)}) conditional(s32[]{:T(128)} %convert_element_type.30, (s32[7]{0:T(128)S(1)}, s32[7]{0:T(128)S(1)}, bf16[8,4,256,256]{3,2,1,0:T(8,128)(2,1)}, bf16[5,4,256,256]{3,2,1,0:T(8,128)(2,1)S(1)}, bf16[8,4,256,256]{3,2,1,0:T(8,128)(2,1)}, /*index=5*/bf16[5,4,256,256]{3,2,1,0:T(8,128)(2,1)}, ...), branch_computations={%region_19.20_spmd, %region_20.21_spmd} | conditional | flops 13158842368 | bytes 97517848 | solution.py:460
  338.0 26.1 %front.3 = bf16[7,14,256,256]{3,2,1,0:T(8,128)(2,1)} custom-call(s32[122]{0:T(128)S(1)} %get-tuple-element.69.s_ref, bf16[7,256,1024]{2,1,0:T(8,128)(2,1)} %get-tuple-element.70.rows_ref, bf16[8,4,256,256]{3,2,1,0:T(8,128)(2,1)} %get-tuple-element.71.refs_0_, bf16[5,4,256,256]{3,2,1,0:T(8,128)(2,1)S(1)} %get-tuple-element.72.refs_1_, ...), custom_call_target="tpu_custom_call" | custom-call | flops 13153337344 | bytes 41943040 | tf_op jit(solution)/shard_map/cond/branch_1_fun/front/pallas_call | solution.py:321
  (98 shorter events, 27.3 us)
Async XLA Ops:
  12.3 59.2 %all-to-all-start = ((bf16[32,256,256]{2,1,0:T(8,128)(2,1)}), bf16[32,256,256]{2,1,0:T(8,128)(2,1)}, u32[]{:S(2)}, u32[]{:S(2)}) async-start(bf16[32,256,256]{2,1,0:T(8,128)(2,1)} %bitcast.66), calls=%async_computation | async-start | bytes 8388608 | tf_op jit(solution)/shard_map/all_to_all | solution.py:38
  30.8 50.4 %copy-start.2 = (bf16[8,32,256]{2,1,0:T(8,128)(2,1)S(1)}, bf16[8,32,256]{2,1,0:T(8,128)(2,1)}, u32[]{:S(2)}) copy-start(bf16[8,32,256]{2,1,0:T(8,128)(2,1)} %get-tuple-element.114) | copy-start | bytes 393220
  71.5 39.3 %all-to-all-start.1 = ((bf16[128,32,256]{2,1,0:T(8,128)(2,1)}), bf16[128,32,256]{2,1,0:T(8,128)(2,1)S(1)}, u32[]{:S(2)}, u32[]{:S(2)}) async-start(bf16[128,32,256]{2,1,0:T(8,128)(2,1)} %bitcast.69), calls=%async_computation.1 | async-start | bytes 4194304 | tf_op jit(solution)/shard_map/all_to_all | solution.py:38
  81.2 31.4 %collective-permute-start.9 = (bf16[32,256]{1,0:T(8,128)(2,1)S(1)}, bf16[32,256]{1,0:T(8,128)(2,1)S(1)}, u32[]{:S(2)}, u32[]{:S(2)}) collective-permute-start(bf16[32,256]{1,0:T(8,128)(2,1)S(1)} %get-tuple-element.159), channel_id=1, source_target_pairs={{0,4},{1,5},{2,6},{3,7},{8,12},{9,13},{10,14},{11,15},{16,20},{17,... | collective-permute-start | bytes 49160 | tf_op jit(solution)/shard_map/ppermute | solution.py:415
  86.5 28.6 %collective-permute-start.8 = (bf16[32,256]{1,0:T(8,128)(2,1)S(1)}, bf16[32,256]{1,0:T(8,128)(2,1)S(1)}, u32[]{:S(2)}, u32[]{:S(2)}) collective-permute-start(bf16[32,256]{1,0:T(8,128)(2,1)S(1)} %get-tuple-element.160), channel_id=1, source_target_pairs={{0,32},{1,33},{2,34},{3,35},{8,40},{9,41},{10,42},{11,43},{16,48},... | collective-permute-start | bytes 49160 | tf_op jit(solution)/shard_map/ppermute | solution.py:415
  87.8 30.2 %collective-permute-start.7 = (bf16[32,256]{1,0:T(8,128)(2,1)S(1)}, bf16[32,256]{1,0:T(8,128)(2,1)S(1)}, u32[]{:S(2)}, u32[]{:S(2)}) collective-permute-start(bf16[32,256]{1,0:T(8,128)(2,1)S(1)} %get-tuple-element.161), channel_id=1, source_target_pairs={{0,36},{1,37},{2,38},{3,39},{8,44},{9,45},{10,46},{11,47},{16,52},... | collective-permute-start | bytes 49160 | tf_op jit(solution)/shard_map/ppermute | solution.py:415
  110.8 25.8 %collective-permute-start.12 = (bf16[8,4,32,256]{3,2,1,0:T(8,128)(2,1)S(1)}, bf16[8,4,32,256]{3,2,1,0:T(8,128)(2,1)S(1)}, u32[]{:S(2)}, u32[]{:S(2)}) collective-permute-start(bf16[8,4,32,256]{3,2,1,0:T(8,128)(2,1)S(1)} %slice.105), channel_id=1, source_target_pairs={{0,6},{1,7},{2,4},{3,5},{4,2},{5,3},{6,0},{7,1},{8,14},{9,15},{10,... | collective-permute-start | bytes 1572872 | tf_op jit(solution)/shard_map/ppermute | solution.py:418
  111.2 25.5 %collective-permute-start.11 = (bf16[8,4,32,256]{3,2,1,0:T(8,128)(2,1)S(1)}, bf16[8,4,32,256]{3,2,1,0:T(8,128)(2,1)S(1)}, u32[]{:S(2)}, u32[]{:S(2)}) collective-permute-start(bf16[8,4,32,256]{3,2,1,0:T(8,128)(2,1)S(1)} %slice.105), channel_id=1, source_target_pairs={{0,4},{1,5},{2,6},{3,7},{4,0},{5,1},{6,2},{7,3},{8,12},{9,13},{10,... | collective-permute-start | bytes 1572872 | tf_op jit(solution)/shard_map/ppermute | solution.py:418
  112.6 24.6 %collective-permute-start.10 = (bf16[8,4,32,256]{3,2,1,0:T(8,128)(2,1)S(1)}, bf16[8,4,32,256]{3,2,1,0:T(8,128)(2,1)S(1)}, u32[]{:S(2)}, u32[]{:S(2)}) collective-permute-start(bf16[8,4,32,256]{3,2,1,0:T(8,128)(2,1)S(1)} %slice.105), channel_id=1, source_target_pairs={{0,2},{1,3},{2,0},{3,1},{4,6},{5,7},{6,4},{7,5},{8,10},{9,11},{10,... | collective-permute-start | bytes 1572872 | tf_op jit(solution)/shard_map/ppermute | solution.py:418
  115.1 4.9 %collective-permute-start.6 = (bf16[32,256]{1,0:T(8,128)(2,1)S(1)}, bf16[32,256]{1,0:T(8,128)(2,1)S(1)}, u32[]{:S(2)}, u32[]{:S(2)}) collective-permute-start(bf16[32,256]{1,0:T(8,128)(2,1)S(1)} %get-tuple-element.162), channel_id=1, source_target_pairs={{0,64},{1,65},{2,66},{3,67},{8,72},{9,73},{10,74},{11,75},{16,80},... | collective-permute-start | bytes 49160 | tf_op jit(solution)/shard_map/ppermute | solution.py:415
  118.0 3.3 collective-permute-start.5
  120.0 3.2 collective-permute-start.4
  121.3 2.7 collective-permute-start.3
  160.0 2.8 collective-permute-start.13
  162.8 110.0 %all-to-all-start.3 = ((bf16[32,256,256]{2,1,0:T(8,128)(2,1)}), bf16[32,256,256]{2,1,0:T(8,128)(2,1)}, u32[]{:S(2)}, u32[]{:S(2)}) async-start(bf16[32,256,256]{2,1,0:T(8,128)(2,1)} %bitcast.67), calls=%async_computation.3 | async-start | bytes 8388608 | tf_op jit(solution)/shard_map/all_to_all | solution.py:38
  168.8 45.9 %copy-start = (bf16[4,8,4,32,256]{4,3,2,1,0:T(8,128)(2,1)}, bf16[4,8,4,32,256]{4,3,2,1,0:T(8,128)(2,1)S(1)}, u32[]{:S(2)}) copy-start(bf16[4,8,4,32,256]{4,3,2,1,0:T(8,128)(2,1)S(1)} %pad_maximum_fusion.3.refs_0_) | copy-start | bytes 6291460
  168.8 48.7 %collective-permute-start.16 = (bf16[4,8,4,32,256]{4,3,2,1,0:T(8,128)(2,1)S(1)}, bf16[4,8,4,32,256]{4,3,2,1,0:T(8,128)(2,1)}, u32[]{:S(2)}, u32[]{:S(2)}) collective-permute-start(bf16[4,8,4,32,256]{4,3,2,1,0:T(8,128)(2,1)S(1)} %pad_maximum_fusion.3.refs_0_), channel_id=1, source_target_pairs={{0,1},{1,0},{2,3},{3,2},{4,5},{5,4},{6,7},{7,6},{8,9},{9,8},{10,11... | collective-permute-start | bytes 6291464 | tf_op jit(solution)/shard_map/ppermute | solution.py:427
  169.5 103.2 %collective-permute-start.14 = (bf16[5,4,256,256]{3,2,1,0:T(8,128)(2,1)}, bf16[5,4,256,256]{3,2,1,0:T(8,128)(2,1)S(1)}, u32[]{:S(2)}, u32[]{:S(2)}) collective-permute-start(bf16[5,4,256,256]{3,2,1,0:T(8,128)(2,1)} %get-tuple-element.126), channel_id=1, source_target_pairs={{0,1},{1,0},{2,3},{3,2},{4,5},{5,4},{6,7},{7,6},{8,9},{9,8},{10,11... | collective-permute-start | bytes 7864328 | tf_op jit(solution)/shard_map/ppermute | solution.py:428
  171.0 101.7 %collective-permute-start.15 = (bf16[5,4,256,256]{3,2,1,0:T(8,128)(2,1)S(1)}, bf16[5,4,256,256]{3,2,1,0:T(8,128)(2,1)}, u32[]{:S(2)}, u32[]{:S(2)}) collective-permute-start(bf16[5,4,256,256]{3,2,1,0:T(8,128)(2,1)S(1)} %copy-done.6), channel_id=1, source_target_pairs={{0,65},{1,64},{2,67},{3,66},{4,69},{5,68},{6,71},{7,70},{8,73},{9,... | collective-permute-start | bytes 7864328 | tf_op jit(solution)/shard_map/ppermute | solution.py:429
  230.1 51.9 %collective-permute-start.18 = (bf16[4,256,1024]{2,1,0:T(8,128)(2,1)}, bf16[4,256,1024]{2,1,0:T(8,128)(2,1)}, u32[]{:S(2)}, u32[]{:S(2)}) collective-permute-start(bf16[4,256,1024]{2,1,0:T(8,128)(2,1)} %get-tuple-element.141), channel_id=1, source_target_pairs={{0,0},{1,64},{2,16},{3,80},{4,32},{5,96},{6,48},{7,112},{8,81},{9,... | collective-permute-start | bytes 6291464 | tf_op jit(solution)/shard_map/ppermute | solution.py:440
  235.0 47.5 %collective-permute-start.19 = (bf16[3,256,1024]{2,1,0:T(8,128)(2,1)}, bf16[3,256,1024]{2,1,0:T(8,128)(2,1)}, u32[]{:S(2)}, u32[]{:S(2)}) collective-permute-start(bf16[3,256,1024]{2,1,0:T(8,128)(2,1)} %get-tuple-element.142), channel_id=1, source_target_pairs={{0,32},{1,96},{2,48},{3,112},{4,0},{5,64},{6,16},{7,80},{8,113},{9... | collective-permute-start | bytes 4718600 | tf_op jit(solution)/shard_map/ppermute | solution.py:440
  277.5 60.5 %collective-permute-start.17 = (bf16[5,4,256,256]{3,2,1,0:T(8,128)(2,1)}, bf16[5,4,256,256]{3,2,1,0:T(8,128)(2,1)}, u32[]{:S(2)}, u32[]{:S(2)}) collective-permute-start(bf16[5,4,256,256]{3,2,1,0:T(8,128)(2,1)} %compact.7), channel_id=1, source_target_pairs={{0,64},{1,65},{2,66},{3,67},{4,68},{5,69},{6,70},{7,71},{8,72},{9,... | collective-permute-start | bytes 7864328 | tf_op jit(solution)/shard_map/ppermute | solution.py:444
  282.1 6.8 %collective-permute-start.20 = (bf16[4,256,1024]{2,1,0:T(8,128)(2,1)}, bf16[4,256,1024]{2,1,0:T(8,128)(2,1)}, u32[]{:S(2)}, u32[]{:S(2)}) collective-permute-start(bf16[4,256,1024]{2,1,0:T(8,128)(2,1)} %collective-permute-done.18), channel_id=1, source_target_pairs={{0,8},{1,9},{2,10},{3,11},{4,12},{5,13},{6,14},{7,15},{8,0},{9,1},... | collective-permute-start | bytes 6291464 | tf_op jit(solution)/shard_map/ppermute | solution.py:441
  282.5 6.4 %collective-permute-start.21 = (bf16[3,256,1024]{2,1,0:T(8,128)(2,1)}, bf16[3,256,1024]{2,1,0:T(8,128)(2,1)}, u32[]{:S(2)}, u32[]{:S(2)}) collective-permute-start(bf16[3,256,1024]{2,1,0:T(8,128)(2,1)} %collective-permute-done.19), channel_id=1, source_target_pairs={{0,8},{1,9},{2,10},{3,11},{4,12},{5,13},{6,14},{7,15},{8,0},{9,1},... | collective-permute-start | bytes 4718600 | tf_op jit(solution)/shard_map/ppermute | solution.py:441
  (4 other events, 54.5 us)

commit v4 on v3

--- a/solution.py
+++ b/solution.py
@@ -302,8 +302,8 @@
                     base = 35 + 42 * f
                     z, e = s_ref[base + b], s_ref[base + 14 + b]
                     ok = row_ok[f] * s_ref[base + 28 + b]
-                    near, far = blocks[2 * f][0, z].astype(f32), blocks[2 * f + 1][0, z].astype(f32)
-                    tile = tile + jnp.where(e == 0, near, far) * ok.astype(f32)
+                    held_tile = jnp.where(e == 0, blocks[2 * f][0, z], blocks[2 * f + 1][0, z])
+                    tile = tile + held_tile.astype(f32) * ok.astype(f32)
                 out_ref[0, b] = tile.astype(bf16)
 
     @pl.when((a == 0) & (row < PANELS))

time: 366 us -> 364 us (level)
  no operation moved by 1% of the time
where the time goes in v4:
time: 364 us; the launch traced here: 362 us
  waiting for transfers between devices  162 us (45%)
  Pallas kernels  109 us (30%)
  starting transfers between devices  57.4 us (16%)
  blocking collectives  22.6 us (6%)
  other arithmetic  5.45 us (1%)
  local copies, waits for them, and re-layouts  4.46 us (1%)
    all_to_all x3, waiting for transfers between devices, exchange(): return lax.all_to_all(x, axes, split_axis=0, concat_axis=0, tiled=True)  61.7 us
    ppermute x1, waiting for transfers between devices, per_device(): lax.ppermute(compact((to_other[:FIRST],), same)[0], ALL, move(1, 0))  49.1 us
    pallas_call x1, Pallas kernels, pivot(): pl.pallas_call(pivot_kernel, out_shape=(jax.ShapeDtypeStruct((PANELS, PAN...  42.2 us
    ppermute x1, waiting for transfers between devices, per_device(): from_01 = lax.ppermute(send_01, ALL, move(0, 1))  35.6 us
    all_to_all x3, starting transfers between devices, exchange(): return lax.all_to_all(x, axes, split_axis=0, concat_axis=0, tiled=True)  24 us
    pallas_call x1, Pallas kernels, front(): pl.pallas_call(front_kernel, out_shape=jax.ShapeDtypeStruct((RL, CL, T, T...  23.9 us
    all_to_all x1, blocking collectives, exchange(): return lax.all_to_all(x, axes, split_axis=0, concat_axis=0, tiled=True)  22.6 us
    pallas_call x2, Pallas kernels, pack(): pl.pallas_call(pack_kernel, out_shape=[jax.ShapeDtypeStruct(shape, bf16)...  19 us
  transfers between devices with their start and end apart: 22, of which 10 were waited for; matrix products, arithmetic and copies ran while one was open for 2% of the time, Pallas kernels for 21%

profile of v4, /device:TPU:8, one launch (start us, length us, event | category | flops | bytes accessed | tf_op | source)
XLA Modules:
  0.0 361.9 jit_solution(15330129368094291152)
XLA Ops:
  3.1 9.2 %pack.3 = bf16[8,4,256,256]{3,2,1,0:T(8,128)(2,1)} custom-call(s32[20]{0:T(128)} %get-tuple-element.173.s_ref, bf16[8,2048,256]{2,1,0:T(8,128)(2,1)} %bitcast.64), custom_call_target="tpu_custom_call" | custom-call | flops 2147483648 | bytes 16777216 | tf_op jit(solution)/shard_map/pack/pallas_call | solution.py:90
  12.3 8.6 %all-to-all-start = ((bf16[32,256,256]{2,1,0:T(8,128)(2,1)}), bf16[32,256,256]{2,1,0:T(8,128)(2,1)}, u32[]{:S(2)}, u32[]{:S(2)}) async-start(bf16[32,256,256]{2,1,0:T(8,128)(2,1)} %bitcast.66), calls=%async_computation | async-start | bytes 8388608 | tf_op jit(solution)/shard_map/all_to_all | solution.py:38
  20.9 9.8 %pack.2 = (bf16[8,4,256,256]{3,2,1,0:T(8,128)(2,1)}, bf16[16,8,32,256]{3,2,1,0:T(8,128)(2,1)}, bf16[8,32,256]{2,1,0:T(8,128)(2,1)}) custom-call(s32[20]{0:T(128)} %get-tuple-element.174.s_ref, bf16[8,2048,256]{2,1,0:T(8,128)(2,1)} %bitcast.65), custom_call_target="tpu_custom_call" | custom-call | flops 2147483648 | bytes 16777216 | tf_op jit(solution)/shard_map/pack/pallas_call | solution.py:90
  30.8 40.7 %all-to-all-done = bf16[32,256,256]{2,1,0:T(8,128)(2,1)} async-done(((bf16[32,256,256]{2,1,0:T(8,128)(2,1)}), bf16[32,256,256]{2,1,0:T(8,128)(2,1)}, u32[]{:S(2)}, u32[]{:S(2)}) %all-to-all-start) | async-done | bytes 4194336 | tf_op jit(solution)/shard_map/all_to_all | solution.py:38
  71.5 9.7 %all-to-all-start.1 = ((bf16[128,32,256]{2,1,0:T(8,128)(2,1)}), bf16[128,32,256]{2,1,0:T(8,128)(2,1)S(1)}, u32[]{:S(2)}, u32[]{:S(2)}) async-start(bf16[128,32,256]{2,1,0:T(8,128)(2,1)} %bitcast.69), calls=%async_computation.1 | async-start | bytes 4194304 | tf_op jit(solution)/shard_map/all_to_all | solution.py:38
  81.2 5.3 %collective-permute-start.9 = (bf16[32,256]{1,0:T(8,128)(2,1)S(1)}, bf16[32,256]{1,0:T(8,128)(2,1)S(1)}, u32[]{:S(2)}, u32[]{:S(2)}) collective-permute-start(bf16[32,256]{1,0:T(8,128)(2,1)S(1)} %get-tuple-element.159), channel_id=1, source_target_pairs={{0,4},{1,5},{2,6},{3,7},{8,12},{9,13},{10,14},{11,15},{16,20},{17,... | collective-permute-start | bytes 49160 | tf_op jit(solution)/shard_map/ppermute | solution.py:415
  89.8 21.0 %all-to-all-done.1 = bf16[128,32,256]{2,1,0:T(8,128)(2,1)S(1)} async-done(((bf16[128,32,256]{2,1,0:T(8,128)(2,1)}), bf16[128,32,256]{2,1,0:T(8,128)(2,1)S(1)}, u32[]{:S(2)}, u32[]{:S(2)}) %all-to-all-start.1) | async-done | bytes 2097184 | tf_op jit(solution)/shard_map/all_to_all | solution.py:38
  112.6 2.3 collective-permute-start.10
  115.1 2.9 collective-permute-start.6
  124.0 6.6 %compact.6 = (bf16[5,4,256,256]{3,2,1,0:T(8,128)(2,1)}, bf16[5,4,256,256]{3,2,1,0:T(8,128)(2,1)}) custom-call(s32[10]{0:T(128)} %pad_add_fusion.5.s_ref, bf16[8,4,256,256]{3,2,1,0:T(8,128)(2,1)} %bitcast.4.refs_0_.refs_1_, bf16[8,4,256,256]{3,2,1,0:T(8,128)(2,1)} %bitcast.4.refs_0_.refs_1_), custom_call_target="tpu_custom_call" | custom-call | bytes 10485760 | tf_op jit(solution)/shard_map/compact/pallas_call | solution.py:114
  130.6 6.0 %collective-permute-done.12 = bf16[8,4,32,256]{3,2,1,0:T(8,128)(2,1)S(1)} collective-permute-done((bf16[8,4,32,256]{3,2,1,0:T(8,128)(2,1)S(1)}, bf16[8,4,32,256]{3,2,1,0:T(8,128)(2,1)S(1)}, u32[]{:S(2)}, u32[]{:S(2)}) %collective-permute-start.12) | collective-permute-done | bytes 524320 | tf_op jit(solution)/shard_map/ppermute | solution.py:418
  137.4 22.6 %all_to_all.20.own_ref = bf16[64,32,256]{2,1,0:T(8,128)(2,1)S(1)} all-to-all(bf16[64,32,256]{2,1,0:T(8,128)(2,1)S(1)} %broadcast_in_dim.182), channel_id=1, replica_groups=mesh['xh'=2,'y1'=2,'y0'=2,'core'=2,'z1'=2,'z0'=2,'xl'=2] {'xh','y1','y0'..., dimensions={0} | all-to-all | bytes 2097152 | tf_op jit(solution)/shard_map/all_to_all | solution.py:38
  162.8 5.7 %all-to-all-start.3 = ((bf16[32,256,256]{2,1,0:T(8,128)(2,1)}), bf16[32,256,256]{2,1,0:T(8,128)(2,1)}, u32[]{:S(2)}, u32[]{:S(2)}) async-start(bf16[32,256,256]{2,1,0:T(8,128)(2,1)} %bitcast.67), calls=%async_computation.3 | async-start | bytes 8388608 | tf_op jit(solution)/shard_map/all_to_all | solution.py:38
  172.5 42.2 %pivot_factor.1 = (bf16[4,1024,256]{2,1,0:T(8,128)(2,1)}, bf16[4,256,256]{2,1,0:T(8,128)(2,1)}, bf16[4,256,256]{2,1,0:T(8,128)(2,1)}) custom-call(s32[1]{0:T(128)} %bitcast.25.core_ref, bf16[64,32,256]{2,1,0:T(8,128)(2,1)} %copy-done.1, bf16[64,32,256]{2,1,0:T(8,128)(2,1)} %collective-permute-done.13.other_ref, f32[4,256,1]{2,1,0:T(8,128)} %reshape.157.shift_ref), custom_call_target="tpu_custom_call" | custom-call | flops 44999999488 | bytes 4194304 | tf_op jit(solution)/shard_map/pivot_factor/pallas_call | solution.py:213
  214.7 2.8 collective-permute-done.16.refs_1_
  217.5 12.7 %panel_rows.1 = (bf16[4,256,1024]{2,1,0:T(8,128)(2,1)}, bf16[3,256,1024]{2,1,0:T(8,128)(2,1)}, bf16[7,256,1024]{2,1,0:T(8,128)(2,1)}) custom-call(s32[16]{0:T(128)} %pad_add_fusion.6.s_ref, bf16[4,8,4,32,256]{4,3,2,1,0:T(8,128)(2,1)} %copy-done, bf16[4,8,4,32,256]{4,3,2,1,0:T(8,128)(2,1)} %collective-permute-done.16.refs_1_, bf16[7,256,1024]{2,1,0:T(8,128)(2,1)} %bitcast.77, ...), custom_call_target="tpu_custom_call" | custom-call | flops 8000000000 | bytes 12582912 | tf_op jit(solution)/shard_map/panel_rows/pallas_call | solution.py:266
  230.1 4.9 %collective-permute-start.18 = (bf16[4,256,1024]{2,1,0:T(8,128)(2,1)}, bf16[4,256,1024]{2,1,0:T(8,128)(2,1)}, u32[]{:S(2)}, u32[]{:S(2)}) collective-permute-start(bf16[4,256,1024]{2,1,0:T(8,128)(2,1)} %get-tuple-element.141), channel_id=1, source_target_pairs={{0,0},{1,64},{2,16},{3,80},{4,32},{5,96},{6,48},{7,112},{8,81},{9,... | collective-permute-start | bytes 6291464 | tf_op jit(solution)/shard_map/ppermute | solution.py:440
  237.2 35.6 %collective-permute-done.14 = bf16[5,4,256,256]{3,2,1,0:T(8,128)(2,1)S(1)} collective-permute-done((bf16[5,4,256,256]{3,2,1,0:T(8,128)(2,1)}, bf16[5,4,256,256]{3,2,1,0:T(8,128)(2,1)S(1)}, u32[]{:S(2)}, u32[]{:S(2)}) %collective-permute-start.14) | collective-permute-done | bytes 2621472 | tf_op jit(solution)/shard_map/ppermute | solution.py:428
  272.7 4.8 %compact.7 = bf16[5,4,256,256]{3,2,1,0:T(8,128)(2,1)} custom-call(s32[5]{0:T(128)S(1)} %bitcast.75, bf16[8,4,256,256]{3,2,1,0:T(8,128)(2,1)} %bitcast.16.refs_0_), custom_call_target="tpu_custom_call" | custom-call | bytes 5242880 | tf_op jit(solution)/shard_map/compact/pallas_call | solution.py:114
  277.5 2.5 collective-permute-start.17
  284.1 4.7 %collective-permute-done.21 = bf16[3,256,1024]{2,1,0:T(8,128)(2,1)} collective-permute-done((bf16[3,256,1024]{2,1,0:T(8,128)(2,1)}, bf16[3,256,1024]{2,1,0:T(8,128)(2,1)}, u32[]{:S(2)}, u32[]{:S(2)}) %collective-permute-start.21) | collective-permute-done | bytes 1572896 | tf_op jit(solution)/shard_map/ppermute | solution.py:441
  288.9 49.1 %collective-permute-done.17 = bf16[5,4,256,256]{3,2,1,0:T(8,128)(2,1)} collective-permute-done((bf16[5,4,256,256]{3,2,1,0:T(8,128)(2,1)}, bf16[5,4,256,256]{3,2,1,0:T(8,128)(2,1)}, u32[]{:S(2)}, u32[]{:S(2)}) %collective-permute-start.17) | collective-permute-done | bytes 2621472 | tf_op jit(solution)/shard_map/ppermute | solution.py:444
  338.0 23.9 %conditional.1 = (bf16[7,14,256,256]{3,2,1,0:T(8,128)(2,1)}) conditional(s32[]{:T(128)} %convert_element_type.30, (s32[7]{0:T(128)S(1)}, s32[7]{0:T(128)S(1)}, bf16[8,4,256,256]{3,2,1,0:T(8,128)(2,1)}, bf16[5,4,256,256]{3,2,1,0:T(8,128)(2,1)S(1)}, bf16[8,4,256,256]{3,2,1,0:T(8,128)(2,1)}, /*index=5*/bf16[5,4,256,256]{3,2,1,0:T(8,128)(2,1)}, ...), branch_computations={%region_19.20_spmd, %region_20.21_spmd} | conditional | flops 13158842368 | bytes 97517848 | solution.py:460
  338.0 23.9 %front.3 = bf16[7,14,256,256]{3,2,1,0:T(8,128)(2,1)} custom-call(s32[122]{0:T(128)S(1)} %get-tuple-element.69.s_ref, bf16[7,256,1024]{2,1,0:T(8,128)(2,1)} %get-tuple-element.70.rows_ref, bf16[8,4,256,256]{3,2,1,0:T(8,128)(2,1)} %get-tuple-element.71.refs_0_, bf16[5,4,256,256]{3,2,1,0:T(8,128)(2,1)S(1)} %get-tuple-element.72.refs_1_, ...), custom_call_target="tpu_custom_call" | custom-call | flops 13153337344 | bytes 41943040 | tf_op jit(solution)/shard_map/cond/branch_1_fun/front/pallas_call | solution.py:321
  (98 shorter events, 27.3 us)
Async XLA Ops:
  12.3 59.2 %all-to-all-start = ((bf16[32,256,256]{2,1,0:T(8,128)(2,1)}), bf16[32,256,256]{2,1,0:T(8,128)(2,1)}, u32[]{:S(2)}, u32[]{:S(2)}) async-start(bf16[32,256,256]{2,1,0:T(8,128)(2,1)} %bitcast.66), calls=%async_computation | async-start | bytes 8388608 | tf_op jit(solution)/shard_map/all_to_all | solution.py:38
  30.8 50.4 %copy-start.2 = (bf16[8,32,256]{2,1,0:T(8,128)(2,1)S(1)}, bf16[8,32,256]{2,1,0:T(8,128)(2,1)}, u32[]{:S(2)}) copy-start(bf16[8,32,256]{2,1,0:T(8,128)(2,1)} %get-tuple-element.114) | copy-start | bytes 393220
  71.5 39.3 %all-to-all-start.1 = ((bf16[128,32,256]{2,1,0:T(8,128)(2,1)}), bf16[128,32,256]{2,1,0:T(8,128)(2,1)S(1)}, u32[]{:S(2)}, u32[]{:S(2)}) async-start(bf16[128,32,256]{2,1,0:T(8,128)(2,1)} %bitcast.69), calls=%async_computation.1 | async-start | bytes 4194304 | tf_op jit(solution)/shard_map/all_to_all | solution.py:38
  81.2 31.4 %collective-permute-start.9 = (bf16[32,256]{1,0:T(8,128)(2,1)S(1)}, bf16[32,256]{1,0:T(8,128)(2,1)S(1)}, u32[]{:S(2)}, u32[]{:S(2)}) collective-permute-start(bf16[32,256]{1,0:T(8,128)(2,1)S(1)} %get-tuple-element.159), channel_id=1, source_target_pairs={{0,4},{1,5},{2,6},{3,7},{8,12},{9,13},{10,14},{11,15},{16,20},{17,... | collective-permute-start | bytes 49160 | tf_op jit(solution)/shard_map/ppermute | solution.py:415
  86.5 28.6 %collective-permute-start.8 = (bf16[32,256]{1,0:T(8,128)(2,1)S(1)}, bf16[32,256]{1,0:T(8,128)(2,1)S(1)}, u32[]{:S(2)}, u32[]{:S(2)}) collective-permute-start(bf16[32,256]{1,0:T(8,128)(2,1)S(1)} %get-tuple-element.160), channel_id=1, source_target_pairs={{0,32},{1,33},{2,34},{3,35},{8,40},{9,41},{10,42},{11,43},{16,48},... | collective-permute-start | bytes 49160 | tf_op jit(solution)/shard_map/ppermute | solution.py:415
  87.8 30.2 %collective-permute-start.7 = (bf16[32,256]{1,0:T(8,128)(2,1)S(1)}, bf16[32,256]{1,0:T(8,128)(2,1)S(1)}, u32[]{:S(2)}, u32[]{:S(2)}) collective-permute-start(bf16[32,256]{1,0:T(8,128)(2,1)S(1)} %get-tuple-element.161), channel_id=1, source_target_pairs={{0,36},{1,37},{2,38},{3,39},{8,44},{9,45},{10,46},{11,47},{16,52},... | collective-permute-start | bytes 49160 | tf_op jit(solution)/shard_map/ppermute | solution.py:415
  110.8 25.8 %collective-permute-start.12 = (bf16[8,4,32,256]{3,2,1,0:T(8,128)(2,1)S(1)}, bf16[8,4,32,256]{3,2,1,0:T(8,128)(2,1)S(1)}, u32[]{:S(2)}, u32[]{:S(2)}) collective-permute-start(bf16[8,4,32,256]{3,2,1,0:T(8,128)(2,1)S(1)} %slice.105), channel_id=1, source_target_pairs={{0,6},{1,7},{2,4},{3,5},{4,2},{5,3},{6,0},{7,1},{8,14},{9,15},{10,... | collective-permute-start | bytes 1572872 | tf_op jit(solution)/shard_map/ppermute | solution.py:418
  111.2 25.5 %collective-permute-start.11 = (bf16[8,4,32,256]{3,2,1,0:T(8,128)(2,1)S(1)}, bf16[8,4,32,256]{3,2,1,0:T(8,128)(2,1)S(1)}, u32[]{:S(2)}, u32[]{:S(2)}) collective-permute-start(bf16[8,4,32,256]{3,2,1,0:T(8,128)(2,1)S(1)} %slice.105), channel_id=1, source_target_pairs={{0,4},{1,5},{2,6},{3,7},{4,0},{5,1},{6,2},{7,3},{8,12},{9,13},{10,... | collective-permute-start | bytes 1572872 | tf_op jit(solution)/shard_map/ppermute | solution.py:418
  112.6 24.6 %collective-permute-start.10 = (bf16[8,4,32,256]{3,2,1,0:T(8,128)(2,1)S(1)}, bf16[8,4,32,256]{3,2,1,0:T(8,128)(2,1)S(1)}, u32[]{:S(2)}, u32[]{:S(2)}) collective-permute-start(bf16[8,4,32,256]{3,2,1,0:T(8,128)(2,1)S(1)} %slice.105), channel_id=1, source_target_pairs={{0,2},{1,3},{2,0},{3,1},{4,6},{5,7},{6,4},{7,5},{8,10},{9,11},{10,... | collective-permute-start | bytes 1572872 | tf_op jit(solution)/shard_map/ppermute | solution.py:418
  115.1 4.9 %collective-permute-start.6 = (bf16[32,256]{1,0:T(8,128)(2,1)S(1)}, bf16[32,256]{1,0:T(8,128)(2,1)S(1)}, u32[]{:S(2)}, u32[]{:S(2)}) collective-permute-start(bf16[32,256]{1,0:T(8,128)(2,1)S(1)} %get-tuple-element.162), channel_id=1, source_target_pairs={{0,64},{1,65},{2,66},{3,67},{8,72},{9,73},{10,74},{11,75},{16,80},... | collective-permute-start | bytes 49160 | tf_op jit(solution)/shard_map/ppermute | solution.py:415
  118.0 3.3 collective-permute-start.5
  120.0 3.2 collective-permute-start.4
  121.3 2.7 collective-permute-start.3
  160.0 2.8 collective-permute-start.13
  162.8 110.0 %all-to-all-start.3 = ((bf16[32,256,256]{2,1,0:T(8,128)(2,1)}), bf16[32,256,256]{2,1,0:T(8,128)(2,1)}, u32[]{:S(2)}, u32[]{:S(2)}) async-start(bf16[32,256,256]{2,1,0:T(8,128)(2,1)} %bitcast.67), calls=%async_computation.3 | async-start | bytes 8388608 | tf_op jit(solution)/shard_map/all_to_all | solution.py:38
  168.8 45.9 %copy-start = (bf16[4,8,4,32,256]{4,3,2,1,0:T(8,128)(2,1)}, bf16[4,8,4,32,256]{4,3,2,1,0:T(8,128)(2,1)S(1)}, u32[]{:S(2)}) copy-start(bf16[4,8,4,32,256]{4,3,2,1,0:T(8,128)(2,1)S(1)} %pad_maximum_fusion.3.refs_0_) | copy-start | bytes 6291460
  168.8 48.7 %collective-permute-start.16 = (bf16[4,8,4,32,256]{4,3,2,1,0:T(8,128)(2,1)S(1)}, bf16[4,8,4,32,256]{4,3,2,1,0:T(8,128)(2,1)}, u32[]{:S(2)}, u32[]{:S(2)}) collective-permute-start(bf16[4,8,4,32,256]{4,3,2,1,0:T(8,128)(2,1)S(1)} %pad_maximum_fusion.3.refs_0_), channel_id=1, source_target_pairs={{0,1},{1,0},{2,3},{3,2},{4,5},{5,4},{6,7},{7,6},{8,9},{9,8},{10,11... | collective-permute-start | bytes 6291464 | tf_op jit(solution)/shard_map/ppermute | solution.py:427
  169.5 103.2 %collective-permute-start.14 = (bf16[5,4,256,256]{3,2,1,0:T(8,128)(2,1)}, bf16[5,4,256,256]{3,2,1,0:T(8,128)(2,1)S(1)}, u32[]{:S(2)}, u32[]{:S(2)}) collective-permute-start(bf16[5,4,256,256]{3,2,1,0:T(8,128)(2,1)} %get-tuple-element.126), channel_id=1, source_target_pairs={{0,1},{1,0},{2,3},{3,2},{4,5},{5,4},{6,7},{7,6},{8,9},{9,8},{10,11... | collective-permute-start | bytes 7864328 | tf_op jit(solution)/shard_map/ppermute | solution.py:428
  171.0 101.7 %collective-permute-start.15 = (bf16[5,4,256,256]{3,2,1,0:T(8,128)(2,1)S(1)}, bf16[5,4,256,256]{3,2,1,0:T(8,128)(2,1)}, u32[]{:S(2)}, u32[]{:S(2)}) collective-permute-start(bf16[5,4,256,256]{3,2,1,0:T(8,128)(2,1)S(1)} %copy-done.6), channel_id=1, source_target_pairs={{0,65},{1,64},{2,67},{3,66},{4,69},{5,68},{6,71},{7,70},{8,73},{9,... | collective-permute-start | bytes 7864328 | tf_op jit(solution)/shard_map/ppermute | solution.py:429
  230.1 51.9 %collective-permute-start.18 = (bf16[4,256,1024]{2,1,0:T(8,128)(2,1)}, bf16[4,256,1024]{2,1,0:T(8,128)(2,1)}, u32[]{:S(2)}, u32[]{:S(2)}) collective-permute-start(bf16[4,256,1024]{2,1,0:T(8,128)(2,1)} %get-tuple-element.141), channel_id=1, source_target_pairs={{0,0},{1,64},{2,16},{3,80},{4,32},{5,96},{6,48},{7,112},{8,81},{9,... | collective-permute-start | bytes 6291464 | tf_op jit(solution)/shard_map/ppermute | solution.py:440
  235.0 47.5 %collective-permute-start.19 = (bf16[3,256,1024]{2,1,0:T(8,128)(2,1)}, bf16[3,256,1024]{2,1,0:T(8,128)(2,1)}, u32[]{:S(2)}, u32[]{:S(2)}) collective-permute-start(bf16[3,256,1024]{2,1,0:T(8,128)(2,1)} %get-tuple-element.142), channel_id=1, source_target_pairs={{0,32},{1,96},{2,48},{3,112},{4,0},{5,64},{6,16},{7,80},{8,113},{9... | collective-permute-start | bytes 4718600 | tf_op jit(solution)/shard_map/ppermute | solution.py:440
  277.5 60.5 %collective-permute-start.17 = (bf16[5,4,256,256]{3,2,1,0:T(8,128)(2,1)}, bf16[5,4,256,256]{3,2,1,0:T(8,128)(2,1)}, u32[]{:S(2)}, u32[]{:S(2)}) collective-permute-start(bf16[5,4,256,256]{3,2,1,0:T(8,128)(2,1)} %compact.7), channel_id=1, source_target_pairs={{0,64},{1,65},{2,66},{3,67},{4,68},{5,69},{6,70},{7,71},{8,72},{9,... | collective-permute-start | bytes 7864328 | tf_op jit(solution)/shard_map/ppermute | solution.py:444
  282.1 6.8 %collective-permute-start.20 = (bf16[4,256,1024]{2,1,0:T(8,128)(2,1)}, bf16[4,256,1024]{2,1,0:T(8,128)(2,1)}, u32[]{:S(2)}, u32[]{:S(2)}) collective-permute-start(bf16[4,256,1024]{2,1,0:T(8,128)(2,1)} %collective-permute-done.18), channel_id=1, source_target_pairs={{0,8},{1,9},{2,10},{3,11},{4,12},{5,13},{6,14},{7,15},{8,0},{9,1},... | collective-permute-start | bytes 6291464 | tf_op jit(solution)/shard_map/ppermute | solution.py:441
  282.5 6.4 %collective-permute-start.21 = (bf16[3,256,1024]{2,1,0:T(8,128)(2,1)}, bf16[3,256,1024]{2,1,0:T(8,128)(2,1)}, u32[]{:S(2)}, u32[]{:S(2)}) collective-permute-start(bf16[3,256,1024]{2,1,0:T(8,128)(2,1)} %collective-permute-done.19), channel_id=1, source_target_pairs={{0,8},{1,9},{2,10},{3,11},{4,12},{5,13},{6,14},{7,15},{8,0},{9,1},... | collective-permute-start | bytes 4718600 | tf_op jit(solution)/shard_map/ppermute | solution.py:441
  (4 other events, 54.5 us)
